TPU v7x, 512 devices: a whole 4x4x16 slice. The times are simulated.
512 devices in a mesh: rep: 8 (over x, z_hi), ty: 8 (over z_lo), tx: 8 (over y, core).
Axes of the slice: x: 4, y: 4, z: 16 (z_hi: 2, z_lo: 8; z = z_hi * 8 + z_lo), core: 2. Of those that a mesh axis runs over, the one named last changes fastest.
Arguments:
- features: bfloat16 [8, 128, 1536, 128], P('rep', 'ty', 'tx'), may hold values from -6 to 6
- fine_grad: bfloat16 [8, 128, 1536, 128], P('rep', 'ty', 'tx'), may hold values from -6 to 6
- conv_weight: bfloat16 [3, 3, 128, 128], replicated, may hold values from -0.1875 to 0.1875
- bottom: bfloat16 [8, 256, 512], P('rep', ('ty', 'tx')), may hold values from -12 to 12
- bottom_grad: bfloat16 [8, 256, 512], P('rep', ('ty', 'tx')), may hold values from -6 to 6
- query_weight: bfloat16 [512, 512], replicated, may hold values from -0.25 to 0.25
- key_weight: bfloat16 [512, 512], replicated, may hold values from -0.25 to 0.25
- value_weight: bfloat16 [512, 512], replicated, may hold values from -0.25 to 0.25
Outputs:
- feature_grad: bfloat16 [8, 128, 1536, 128], P('rep', 'ty', 'tx')
- conv_weight_grad: float32 [3, 3, 128, 128], replicated
- bottom_input_grad: bfloat16 [8, 256, 512], P('rep', ('ty', 'tx'))
- projection_grad: float32 [512, 1536], P(('ty', 'tx'))
All inputs are finite; a program needn't handle non-finite values.
Results may differ from a plain program's by a relative error of at most 0.015.
The roundings to bfloat16 on the way count: a program that leaves them out, or rounds other values in their place, can miss the bound.
Values may be sent and summed in bfloat16 or wider, within the bound.
A program may use at most 64 MiB of HBM per device.

v0:
```python
import math

import jax
import jax.numpy as jnp
from jax import lax
from jax.sharding import PartitionSpec as P

HEAD_DIM = 64


def padded_2(array, sides, width):
    for axis, dim in sides:
        count, length = (lax.axis_size(axis), array.shape[dim])
        up = [(i, (i + 1) % count) for i in range(count - 1)]
        down = [(j, i) for i, j in up]
        last = lax.slice_in_dim(array, length - width, length, axis=dim)
        initial = lax.slice_in_dim(array, 0, width, axis=dim)
        before = lax.ppermute(last, axis, up)
        after = lax.ppermute(initial, axis, down)
        array = jnp.concatenate([before, array, after], axis=dim)
    return array


def attention_back(query, key_rows, value_rows, upstream, head_size):
    rows = query.shape[0]
    count = key_rows.shape[0]
    width = query.shape[1]
    head_count = width // head_size
    query_heads = query.reshape(rows, head_count, head_size)
    key_heads = key_rows.reshape(count, head_count, head_size)
    value_heads = value_rows.reshape(count, head_count, head_size)
    upstream_heads = upstream.reshape(rows, head_count, head_size)
    score_scale = 1.0 / math.sqrt(head_size)
    scores = (
        jnp.einsum("rhe,she->hrs", query_heads, key_heads, preferred_element_type=jnp.float32)
        * score_scale
    )
    highest = jnp.max(scores, axis=-1, keepdims=True)
    expos = jnp.exp(scores - highest)
    probs = expos / jnp.sum(expos, axis=-1, keepdims=True)
    probs_low = probs.astype(jnp.bfloat16)
    dprobs = jnp.einsum(
        "rhe,she->hrs", upstream_heads, value_heads, preferred_element_type=jnp.float32
    )
    value_grad = jnp.einsum(
        "hrs,rhe->she", probs_low, upstream_heads, preferred_element_type=jnp.float32
    )
    dscores = probs * (dprobs - jnp.sum(dprobs * probs, axis=-1, keepdims=True))
    dscores_low = (dscores * score_scale).astype(jnp.bfloat16)
    query_grad = jnp.einsum(
        "hrs,she->rhe", dscores_low, key_heads, preferred_element_type=jnp.float32
    )
    key_grad = jnp.einsum(
        "hrs,rhe->she", dscores_low, query_heads, preferred_element_type=jnp.float32
    )
    return (
        query_grad.reshape(rows, width),
        key_grad.reshape(count, width),
        value_grad.reshape(count, width),
    )


def shards(
    features, fine_grad, conv_weight, bottom, bottom_grad, query_weight, key_weight, value_weight
):
    image = features[0]
    upstream = fine_grad[0]
    rows, cols, chans = image.shape
    image_f = image.astype(jnp.float32)
    gate_value = jax.nn.sigmoid(image_f)
    activation = (image_f * gate_value).astype(jnp.bfloat16)
    act_slope = gate_value * (1.0 + image_f * (1.0 - gate_value))
    padded = padded_2(jnp.stack((upstream, activation)), (("ty", 1), ("tx", 2)), 1)
    grad_pad = padded[0]
    act_pad = padded[1]
    act_cat = jnp.concatenate(
        [
            act_pad[row_off : row_off + rows, col_off : col_off + cols]
            for row_off in range(3)
            for col_off in range(3)
        ],
        axis=-1,
    ).reshape(rows * cols, 9 * chans)
    weight_part = lax.dot_general(
        act_cat,
        upstream.reshape(rows * cols, chans),
        (((0,), (0,)), ((), ())),
        preferred_element_type=jnp.float32,
    )
    conv_weight_grad = lax.psum(weight_part, ("rep", "ty", "tx")).reshape(3, 3, chans, chans)
    grad_cat = jnp.concatenate(
        [
            grad_pad[2 - row_off : 2 - row_off + rows, 2 - col_off : 2 - col_off + cols]
            for row_off in range(3)
            for col_off in range(3)
        ],
        axis=-1,
    ).reshape(rows * cols, 9 * chans)
    flipped = conv_weight.transpose(0, 1, 3, 2).reshape(9 * chans, chans)
    act_grad = jnp.dot(grad_cat, flipped, preferred_element_type=jnp.float32).reshape(
        rows, cols, chans
    )
    feature_grad = (upstream.astype(jnp.float32) + act_slope * act_grad).astype(jnp.bfloat16)
    tokens = bottom[0]
    token_grad = bottom_grad[0]
    local_rows = tokens.shape[0]
    width = tokens.shape[1]
    group_index = lax.axis_index(("ty", "tx"))
    joined = jnp.concatenate((query_weight, key_weight, value_weight), axis=1)
    all_tokens, all_grads = (
        lax.all_gather(tokens, ("ty", "tx"), axis=0, tiled=True),
        lax.all_gather(token_grad, ("ty", "tx"), axis=0, tiled=True),
    )
    projected = jnp.dot(all_tokens, joined, preferred_element_type=jnp.float32).astype(jnp.bfloat16)
    query_grad, key_grad, value_grad = attention_back(
        projected[:, :width],
        projected[:, width : 2 * width],
        projected[:, 2 * width :],
        all_grads,
        HEAD_DIM,
    )
    all_proj_grads = jnp.concatenate((query_grad, key_grad, value_grad), axis=1).astype(
        jnp.bfloat16
    )
    own_grads = lax.dynamic_slice_in_dim(all_proj_grads, group_index * local_rows, local_rows, 0)
    back = lax.dot_general(
        own_grads, joined, (((1,), (1,)), ((), ())), preferred_element_type=jnp.float32
    )
    token_out = (token_grad.astype(jnp.float32) + back).astype(jnp.bfloat16)
    slice_rows = width // lax.axis_size(("ty", "tx"))
    token_cols = lax.dynamic_slice_in_dim(all_tokens, group_index * slice_rows, slice_rows, 1)
    proj_part = lax.dot_general(
        token_cols, all_proj_grads, (((0,), (0,)), ((), ())), preferred_element_type=jnp.float32
    )
    projection_grad = lax.psum(proj_part.astype(jnp.bfloat16), "rep").astype(jnp.float32)
    return (feature_grad[None], conv_weight_grad, token_out[None], projection_grad)


def solution(mesh):
    in_specs = (
        P("rep", "ty", "tx", None),
        P("rep", "ty", "tx", None),
        P(),
        P("rep", ("ty", "tx"), None),
        P("rep", ("ty", "tx"), None),
        P(),
        P(),
        P(),
    )
    out_specs = (
        P("rep", "ty", "tx", None),
        P(),
        P("rep", ("ty", "tx"), None),
        P(("ty", "tx"), None),
    )
    return jax.shard_map(shards, mesh=mesh, in_specs=in_specs, out_specs=out_specs, check_vma=False)
```

profile of v0, /device:TPU:1, one launch (start us, length us, event | category | flops | bytes accessed | tf_op | source)
XLA Modules:
  0.0 835.6 jit_solution(14946807028171203147)
XLA Ops:
  7.2 1.6 fusion.20
  8.9 0.7 pad_maximum_fusion.3
  9.6 1.3 collective-permute-start.1
  10.9 5.6 collective-permute-start
  16.6 130.1 %all-gather.1 = bf16[1,256,512]{2,0,1:T(2,128)(2,1)} all-gather(bf16[1,4,512]{2,0,1:T(2,128)(2,1)S(1)} %copy.30), channel_id=3, replica_groups=mesh['rep'=8,'ty'=8,'tx'=8] {'ty','tx'}, dimensions={1}, use_global_device_ids=true | all-gather | bytes 266240 | tf_op jit(solution)/shard_map/all_gather | solution.py:112
  146.7 1.2 copy.31
  148.0 113.8 %all-gather = bf16[1,256,512]{2,0,1:T(2,128)(2,1)S(1)} all-gather(bf16[1,4,512]{2,0,1:T(2,128)(2,1)S(1)} %copy.29), channel_id=2, replica_groups=mesh['rep'=8,'ty'=8,'tx'=8] {'ty','tx'}, dimensions={1}, use_global_device_ids=true | all-gather | bytes 266240 | tf_op jit(solution)/shard_map/all_gather | solution.py:111
  261.8 1.3 constant_dynamic-update-slice_fusion.1
  263.1 1.1 constant_dynamic-update-slice_fusion
  264.1 0.6 fusion.2
  264.8 0.9 fusion.39
  265.7 3.2 fusion.40
  268.9 2.9 fusion.42
  271.8 1.2 convolution_convert_fusion.2
  272.9 5.0 convolution_convert_fusion.3
  277.9 4.9 convolution_convert_fusion.4
  282.9 1.1 constant_dynamic-slice_fusion
  284.1 1.2 pad_maximum_fusion.1
  285.5 1.4 fusion.23
  287.0 0.7 pad_maximum_fusion.7
  287.7 2.1 collective-permute-start.3
  289.8 3.5 collective-permute-start.2
  293.3 67.8 %psum.15 = bf16[8,1536]{1,0:T(8,128)(2,1)S(1)} all-reduce(bf16[8,1536]{1,0:T(8,128)(2,1)S(1)} %convolution_convert_fusion.1), channel_id=1, replica_groups=mesh['rep'=8,'ty'=8,'tx'=8] {'rep'}, use_global_device_ids=true, to_apply=%region_4.0 | all-reduce | flops 12288 | bytes 49152 | tf_op jit(solution)/shard_map/psum | solution.py:135
  361.0 1.2 copy.28
  362.2 0.6 convert_element_type.61
  362.8 1.8 pad_maximum_fusion
  368.8 0.3 slice_dynamic-update-slice_fusion.11
  369.1 0.8 slice_dynamic-update-slice_fusion
  370.1 3.1 fusion.41
  373.3 6.2 fusion.21
  379.5 447.3 %all-reduce.2.cloned.1.call-done = f32[3,3,128,128]{3,2,1,0:T(8,128)} async-done(((f32[3,3,128,128]{3,2,1,0:T(8,128)}), f32[3,3,128,128]{3,2,1,0:T(8,128)}) %all-reduce.2.cloned.1.call-update) | async-done | bytes 589840 | tf_op jit(solution)/shard_map/psum | solution.py:90
  826.8 1.9 copy.64
  (45 shorter events, 4.8 us)
Async XLA Ops:
  7.2 1.7 copy-start
  7.2 9.4 %copy-start.6 = (bf16[1,4,512]{2,1,0:T(4,128)(2,1)S(1)}, bf16[1,4,512]{2,1,0:T(4,128)(2,1)}, u32[]{:S(2)}) copy-start(bf16[1,4,512]{2,1,0:T(4,128)(2,1)} %param.12) | copy-start | bytes 12292
  7.2 819.6 %all-reduce.2.cloned.1.call-start = ((), (), s32[]{:S(2)}) async-start(), calls=%async_computation | async-start | bytes 1179648 | tf_op jit(solution)/shard_map/psum | solution.py:90
  7.2 9.3 %copy-start.3 = (bf16[512,512]{1,0:T(8,128)(2,1)S(1)}, bf16[512,512]{1,0:T(8,128)(2,1)}, u32[]{:S(2)}) copy-start(bf16[512,512]{1,0:T(8,128)(2,1)} %param.13) | copy-start | bytes 1572868
  8.9 139.0 %copy-start.7 = (bf16[1,4,512]{2,1,0:T(4,128)(2,1)S(1)}, bf16[1,4,512]{2,1,0:T(4,128)(2,1)}, u32[]{:S(2)}) copy-start(bf16[1,4,512]{2,1,0:T(4,128)(2,1)} %param.11) | copy-start | bytes 12292
  9.6 277.3 %collective-permute-start.1 = (bf16[2,1,192,128]{3,2,1,0:T(8,128)(2,1)}, bf16[2,1,192,128]{3,2,1,0:T(8,128)(2,1)S(1)}, u32[]{:S(2)}, u32[]{:S(2)}) collective-permute-start(bf16[2,1,192,128]{3,2,1,0:T(8,128)(2,1)} %get-tuple-element.9), channel_id=1, source_target_pairs={{8,0},{16,8},{24,16},{32,24},{40,32},{48,40},{56,48},{9,1},{17,9},... | collective-permute-start | bytes 294920 | tf_op jit(solution)/shard_map/ppermute | solution.py:19
  10.9 276.1 %collective-permute-start = (bf16[2,1,192,128]{3,2,1,0:T(8,128)(2,1)}, bf16[2,1,192,128]{3,2,1,0:T(8,128)(2,1)}, u32[]{:S(2)}, u32[]{:S(2)}) collective-permute-start(bf16[2,1,192,128]{3,2,1,0:T(8,128)(2,1)} %get-tuple-element.8), channel_id=1, source_target_pairs={{0,8},{8,16},{16,24},{24,32},{32,40},{40,48},{48,56},{1,9},{9,17},... | collective-permute-start | bytes 294920 | tf_op jit(solution)/shard_map/ppermute | solution.py:18
  261.8 3.0 copy-start.1
  268.9 2.9 copy-start.8
  272.9 5.0 copy-start.4
  287.7 75.2 %collective-permute-start.3 = (bf16[2,18,1,128]{3,2,1,0:T(2,128)(2,1)S(1)}, bf16[2,18,1,128]{3,2,1,0:T(2,128)(2,1)S(1)}, u32[]{:S(2)}, u32[]{:S(2)}) collective-permute-start(bf16[2,18,1,128]{3,2,1,0:T(2,128)(2,1)S(1)} %get-tuple-element.7), channel_id=1, source_target_pairs={{1,0},{2,1},{3,2},{4,3},{5,4},{6,5},{7,6},{9,8},{10,9},{11,10},{12... | collective-permute-start | bytes 27656 | tf_op jit(solution)/shard_map/ppermute | solution.py:19
  289.8 73.1 %collective-permute-start.2 = (bf16[2,18,1,128]{3,2,1,0:T(2,128)(2,1)S(1)}, bf16[2,18,1,128]{3,2,1,0:T(2,128)(2,1)S(1)}, u32[]{:S(2)}, u32[]{:S(2)}) collective-permute-start(bf16[2,18,1,128]{3,2,1,0:T(2,128)(2,1)S(1)} %get-tuple-element.6), channel_id=1, source_target_pairs={{0,1},{1,2},{2,3},{3,4},{4,5},{5,6},{6,7},{8,9},{9,10},{10,11},{11... | collective-permute-start | bytes 27656 | tf_op jit(solution)/shard_map/ppermute | solution.py:18
  370.1 3.1 copy-start.5
  370.1 3.2 copy-start.2
Sparse Core Ops, SparseCore 0:
  373.4 453.3 all-reduce.1
where the time goes:
time: 836 us
  waiting for transfers between devices  447 us (53%)
  blocking collectives  312 us (37%)
  matrix products  28.9 us (3%)
  between operations  14.3 us (2%)
  local copies, waits for them, and re-layouts  14.2 us (2%)
  starting transfers between devices  12.5 us (1%)
    psum x1, waiting for transfers between devices, shards(): lax.psum(weight_part, ('rep', 'ty', 'tx')).reshape(3, 3, chans, chans)  447 us
    all_gather x1, blocking collectives, shards(): lax.all_gather(token_grad, ('ty', 'tx'), axis=0, tiled=True)  130 us
    all_gather x1, blocking collectives, shards(): lax.all_gather(tokens, ('ty', 'tx'), axis=0, tiled=True)  114 us
    psum x1, blocking collectives, shards(): lax.psum(proj_part.astype(jnp.bfloat16), 'rep').astype(jnp.float32)  67.8 us
  transfers between devices with their start and end apart: 5, of which 1 were waited for; matrix products, arithmetic and copies ran while one was open for 4% of the time, Pallas kernels for 0%

commit v1 on v0

v1 whole, which is shorter than its diff:
```python
import dataclasses
import functools

import jax
import jax.numpy as jnp
from jax import lax
from jax.experimental import pallas as pl
from jax.experimental.pallas import tpu as pltpu
from jax.sharding import PartitionSpec as P

HEAD_DIM = 64
LANES = 128
TILE = 16
MESH = pl.DeviceIdType.MESH
BF16 = jnp.bfloat16
F32 = jnp.float32

NN = (((1,), (0,)), ((), ()))
NT = (((1,), (1,)), ((), ()))
TN = (((0,), (0,)), ((), ()))


def dot(a, b, dims):
    return lax.dot_general(a, b, dims, preferred_element_type=F32)


@dataclasses.dataclass(frozen=True)
class Dims:
    x: int
    zh: int
    ty: int
    tx: int
    rows: int
    cols: int
    tok: int
    width: int

    @property
    def z(self):
        return self.zh * self.ty

    @property
    def part(self):
        return 9 * LANES // self.tx

    @property
    def owners(self):
        return 9 if self.z >= 9 else 3

    @property
    def piece(self):
        return self.part // self.owners

    @property
    def tokens(self):
        return self.ty * self.tx * self.tok

    def owner(self, j):
        return j * self.z // self.owners


def message_slots(d):
    slots = {}
    count = 0
    for name, n in (
        ("row", 2),
        ("col", 6),
        ("tok_z", d.ty),
        ("tok_t", d.tx),
        ("scatter", d.tx),
        ("sum_x", d.x),
        ("own", max(d.owners, d.z)),
        ("cast", max(d.owners, d.z)),
        ("gather", d.tx),
        ("proj_z", d.zh),
        ("proj_x", d.x),
    ):
        slots[name] = count
        count += n
    return slots, count


def kernel(
    d,
    features,
    fine_grad,
    conv_weight,
    bottom,
    bottom_grad,
    query_weight,
    key_weight,
    value_weight,
    feature_out,
    weight_out,
    token_out,
    proj_out,
    feat_v,
    grad_v,
    shifted,
    taps,
    proj_w,
    out_v,
    acc,
    part_v,
    scatter_v,
    sum_v,
    total_v,
    own_v,
    fin,
    col_send,
    col_recv,
    col_halo,
    tok_v,
    pack_v,
    gath,
    wide,
    tok_all,
    qkv,
    pgrad,
    pz_v,
    px_v,
    local_sem,
    send_sem,
    recv_sem,
):
    slots, _ = message_slots(d)
    rows, cols = d.rows, d.cols
    rep, ty, tx = (lax.axis_index(a) for a in ("rep", "ty", "tx"))
    x, zh = rep // d.zh, rep % d.zh
    z = zh * d.ty + ty

    def at_x(i):
        return (lax.rem(x + i, d.x) * d.zh + zh, ty, tx)

    def at_z(k):
        return (x * d.zh + k // d.ty, lax.rem(k, d.ty), tx)

    def at_tx(t):
        return (rep, ty, t)

    def at_ty(t):
        return (rep, t, tx)

    def send(src, dst, name, out_index, in_index, device):
        return pltpu.make_async_remote_copy(
            src_ref=src,
            dst_ref=dst,
            send_sem=send_sem.at[slots[name] + out_index],
            recv_sem=recv_sem.at[slots[name] + in_index],
            device_id=device,
            device_id_type=MESH,
        )

    sent = []

    def start(copy, when=None):
        sent.append((when, copy))
        if when is None:
            copy.start()
        else:
            pl.when(when)(copy.start)

    def local(src, dst, i):
        copy = pltpu.make_async_copy(src, dst, local_sem.at[i])
        copy.start()
        return copy

    in_tok = [local(bottom.at[0], tok_v.at[0], 0), local(bottom_grad.at[0], tok_v.at[1], 1)]
    in_grad = local(fine_grad.at[0], grad_v.at[pl.ds(1, rows)], 2)
    in_feat = local(features.at[0], feat_v, 3)
    in_proj = [
        local(w, proj_w.at[i], 4 + i) for i, w in enumerate((query_weight, key_weight, value_weight))
    ]
    in_taps = [
        local(conv_weight.at[k // 3, k % 3], taps.at[:, pl.ds(k * LANES, LANES)], 7 + k)
        for k in range(9)
    ]

    barrier = pltpu.get_barrier_semaphore()
    peers = [at_tx(lax.rem(tx + i, d.tx)) for i in range(1, d.tx)]
    peers += [at_x(i) for i in range(1, d.x)]
    peers += [at_z(lax.rem(z + i, d.z)) for i in range(1, d.z)]
    for dy in (1, d.ty - 1):
        for dx in (1, d.tx - 1):
            peers.append((rep, lax.rem(ty + dy, d.ty), lax.rem(tx + dx, d.tx)))
    for peer in peers:
        pl.semaphore_signal(barrier, inc=1, device_id=peer, device_id_type=MESH)

    blocks = d.width // LANES
    for i, copy in enumerate(in_tok):
        copy.wait()
        mine = tok_v[i].astype(F32)
        for c in range(blocks):
            pack_v[i, pl.ds(c, d.tok, stride=blocks), :] = mine[:, c * LANES : (c + 1) * LANES]
        gath[i, tx, ty] = pack_v[i].astype(BF16)
    in_grad.wait()
    lane_rows = lax.broadcasted_iota(jnp.int32, (rows, TILE, LANES), 1)
    for side, base, row in ((0, 0, 0), (1, cols - TILE, TILE - 1)):
        edge = grad_v[1 : rows + 1, base : base + TILE, :].astype(F32)
        edge = jnp.sum(jnp.where(lane_rows == row, edge, 0.0), axis=1)
        col_send[side] = edge.astype(BF16)

    pl.semaphore_wait(barrier, len(peers))

    up, down = ty > 0, ty < d.ty - 1
    left, right = tx > 0, tx < d.tx - 1
    upper, lower = lax.rem(ty + d.ty - 1, d.ty), lax.rem(ty + 1, d.ty)
    row_up = send(grad_v.at[1], grad_v.at[rows + 1], "row", 0, 1, at_ty(upper))
    row_down = send(grad_v.at[rows], grad_v.at[0], "row", 1, 0, at_ty(lower))
    start(row_up, up)
    start(row_down, down)
    arrivals = []
    for side, there, out_ok, in_ok in (
        (0, lax.rem(tx + d.tx - 1, d.tx), left, right),
        (1, lax.rem(tx + 1, d.tx), right, left),
    ):
        for dy, there_y, out_y, in_y in (
            (0, upper, up, down),
            (1, ty, True, True),
            (2, lower, down, up),
        ):
            copy = send(
                col_send.at[side],
                col_recv.at[1 - side, 2 - dy],
                "col",
                side * 3 + dy,
                (1 - side) * 3 + 2 - dy,
                (rep, there_y, there),
            )
            start(copy, jnp.logical_and(out_ok, out_y))
            arrivals.append((jnp.logical_and(in_ok, in_y), copy, 1 - side, 2 - dy))

    def tok_z(i):
        return send(
            gath.at[:, tx, ty], gath.at[:, tx, ty], "tok_z", i, i, at_ty(lax.rem(ty + i, d.ty))
        )

    for i in range(1, d.ty):
        start(tok_z(i))

    col_halo[...] = jnp.zeros_like(col_halo)

    @pl.when(jnp.logical_not(up))
    def _():
        grad_v[0] = jnp.zeros((cols, LANES), BF16)

    @pl.when(jnp.logical_not(down))
    def _():
        grad_v[rows + 1] = jnp.zeros((cols, LANES), BF16)

    pl.when(up)(row_down.wait_recv)
    pl.when(down)(row_up.wait_recv)
    for ok, copy, side, place in arrivals:

        @pl.when(ok)
        def _(copy=copy, side=side, place=place):
            copy.wait_recv()
            tile = col_recv[side, place].astype(F32)
            if place == 0:
                col_halo[side, 0:1] = tile[rows - 1 : rows]
            elif place == 1:
                col_halo[side, 1 : rows + 1] = tile
            else:
                col_halo[side, rows + 1 : rows + 2] = tile[0:1]

    for i in range(1, d.ty):
        tok_z(i).wait_recv()

    def tok_t(i):
        return send(gath.at[:, tx], gath.at[:, tx], "tok_t", i, i, at_tx(lax.rem(tx + i, d.tx)))

    for i in range(1, d.tx):
        start(tok_t(i))

    col_index = lax.broadcasted_iota(jnp.int32, (cols, LANES), 0)

    def shift_row(r, carry):
        line = grad_v[r]
        wide_line = line.astype(F32)
        before = jnp.where(col_index == 0, col_halo[0, pl.ds(r, 1)], pltpu.roll(wide_line, 1, 0))
        after = jnp.where(
            col_index == cols - 1, col_halo[1, pl.ds(r, 1)], pltpu.roll(wide_line, cols - 1, 0)
        )
        shifted[r, :, 0:LANES] = after.astype(BF16)
        shifted[r, :, LANES : 2 * LANES] = line
        shifted[r, :, 2 * LANES :] = before.astype(BF16)
        return carry

    lax.fori_loop(0, rows + 2, shift_row, 0)
    in_feat.wait()

    group = 4
    pixels = group * cols

    def neighbours(r):
        return jnp.concatenate(
            [
                shifted[pl.ds(r + 2 - ky, group)].reshape(pixels, 3 * LANES)
                for ky in range(3)
            ],
            axis=-1,
        )

    acc[...] = jnp.zeros_like(acc)

    def weight_step(i, carry):
        value = feat_v[pl.ds(i * group, group)].reshape(pixels, LANES).astype(F32)
        active = (value * jax.nn.sigmoid(value)).astype(BF16)
        acc[...] += dot(active, neighbours(i * group), TN)
        return carry

    lax.fori_loop(0, rows // group, weight_step, 0)
    for k in range(9):
        part_v[k * LANES : (k + 1) * LANES, :] = acc[:, k * LANES : (k + 1) * LANES].astype(BF16)

    def slab(t):
        return pl.ds(pl.multiple_of(t * d.part, TILE), d.part)

    def scatter(i):
        there = lax.rem(tx + i, d.tx)
        return send(part_v.at[slab(there)], scatter_v.at[i], "scatter", i, i, at_tx(there))

    for i in range(1, d.tx):
        start(scatter(i))

    for copy in in_taps:
        copy.wait()

    def feature_step(i, carry):
        here = pl.ds(i * group, group)
        value = feat_v[here].reshape(pixels, LANES).astype(F32)
        gate = jax.nn.sigmoid(value)
        slope = gate * (1.0 + value * (1.0 - gate))
        act_grad = dot(neighbours(i * group), taps[...], NT)
        upstream = grad_v[pl.ds(i * group + 1, group)].reshape(pixels, LANES).astype(F32)
        out_v[here] = (upstream + slope * act_grad).astype(BF16).reshape(group, cols, LANES)
        return carry

    lax.fori_loop(0, rows // group, feature_step, 0)
    out_feature = local(out_v, feature_out.at[0], 16)

    for i in range(1, d.tx):
        scatter(i).wait_recv()
    total = part_v[slab(tx)].astype(F32)
    for i in range(1, d.tx):
        total = total + scatter_v[i].astype(F32)
    sum_v[x] = total.astype(BF16)

    def sum_x(i):
        return send(sum_v.at[x], sum_v.at[x], "sum_x", i, i, at_x(i))

    for i in range(1, d.x):
        start(sum_x(i))

    for i in range(1, d.tx):
        tok_t(i).wait_recv()
    for i in range(2):
        wide[...] = gath[i].reshape(d.tokens * blocks, LANES).astype(F32)
        for c in range(blocks):
            tok_all[i, :, c * LANES : (c + 1) * LANES] = wide[
                pl.ds(c, d.tokens, stride=blocks), :
            ].astype(BF16)
    for i, copy in enumerate(in_proj):
        copy.wait()
        qkv[:, i * d.width : (i + 1) * d.width] = dot(tok_all[0], proj_w[i], NN).astype(BF16)

    for i in range(1, d.x):
        sum_x(i).wait_recv()
    total = sum_v[0].astype(F32)
    for i in range(1, d.x):
        total = total + sum_v[i].astype(F32)
    total_v[...] = total.astype(BF16)

    def own(j):
        return send(
            total_v.at[pl.ds(j * d.piece, d.piece)],
            own_v.at[z],
            "own",
            j,
            z,
            at_z(d.owner(j)),
        )

    def own_from(k):
        return send(total_v.at[pl.ds(0, d.piece)], own_v.at[k], "own", 0, k, at_z(k))

    for j in range(d.owners):
        start(own(j), z != d.owner(j))

    lane = lax.broadcasted_iota(jnp.int32, (d.tokens, LANES), 1)
    low = lane < HEAD_DIM
    scale = 1.0 / HEAD_DIM**0.5

    def head_pair(p, carry):
        def block(ref, offset):
            return ref[:, pl.ds(pl.multiple_of(offset + p * LANES, LANES), LANES)]

        def halves(v):
            zero = jnp.zeros_like(v)
            return jnp.concatenate([jnp.where(low, v, zero), jnp.where(low, zero, v)], axis=0)

        key = block(qkv, d.width)
        value = block(qkv, 2 * d.width)
        query2 = halves(block(qkv, 0))
        upstream2 = halves(block(tok_all.at[1], 0))
        scores = dot(key, query2, NT) * scale
        expos = jnp.exp(scores - jnp.max(scores, axis=0, keepdims=True))
        probs = expos / jnp.sum(expos, axis=0, keepdims=True)
        dprobs = dot(value, upstream2, NT)
        dscores = probs * (dprobs - jnp.sum(dprobs * probs, axis=0, keepdims=True))
        dscores_low = (dscores * scale).astype(BF16)
        value_grad = dot(probs.astype(BF16), upstream2, NN)
        key_grad = dot(dscores_low, query2, NN)
        both = dot(dscores_low, key, TN)
        query_grad = jnp.where(low, both[: d.tokens], both[d.tokens :])
        for i, g in enumerate((query_grad, key_grad, value_grad)):
            here = pl.ds(pl.multiple_of(i * d.width + p * LANES, LANES), LANES)
            pgrad[:, here] = g.astype(BF16)
        return carry

    pairs = d.width // LANES
    lax.fori_loop(0, pairs // 2, head_pair, 0)

    def cast(j, k):
        here = fin.at[tx, pl.ds(j * d.piece, d.piece)]
        return send(here, here, "cast", k, j, at_z(k))

    for j in range(d.owners):

        @pl.when(z == d.owner(j))
        def _(j=j):
            own_v[z] = total_v[j * d.piece : (j + 1) * d.piece]
            for k in range(d.z):
                if k != d.owner(j):
                    own_from(k).wait_recv()
            whole = own_v[0].astype(F32)
            for k in range(1, d.z):
                whole = whole + own_v[k].astype(F32)
            fin[tx, j * d.piece : (j + 1) * d.piece] = whole.astype(BF16)
            for k in range(d.z):
                if k != d.owner(j):
                    cast(j, k).start()

    lax.fori_loop(pairs // 2, pairs, head_pair, 0)

    place = (tx * d.ty + ty) * d.tok
    channels = d.width // (d.ty * d.tx)
    first = (ty * d.tx + tx) * channels
    pick_row = lax.broadcasted_iota(jnp.int32, (2 * 8, d.width), 0)
    pick_col = lax.broadcasted_iota(jnp.int32, (2 * 8, d.width), 1)
    pick = jnp.logical_and(pick_col == first + pick_row, pick_row < 8).astype(F32).astype(BF16)
    columns = dot(pick, tok_all[0], NT)
    own_row = lax.broadcasted_iota(jnp.int32, (2 * 8, d.tokens), 0)
    own_col = lax.broadcasted_iota(jnp.int32, (2 * 8, d.tokens), 1)
    picked = jnp.where(
        own_row < 8, columns, (own_col == place + own_row - 8).astype(F32)
    ).astype(BF16)
    both = dot(picked, pgrad[...], NN)
    half = 3 * d.width // 2
    pz_v[zh] = jnp.concatenate([both[:8, :half], both[:8, half:]], axis=0).astype(BF16)
    proj_z = send(pz_v.at[zh], pz_v.at[zh], "proj_z", 0, 0, at_z(lax.rem(z + d.ty, d.z)))
    start(proj_z)
    own_grads = both[8:].astype(BF16)
    back = jnp.zeros((8, d.width), F32)
    for i in range(3):
        back = back + dot(own_grads[:, i * d.width : (i + 1) * d.width], proj_w[i], NT)
    token_out[0] = (tok_v[1].astype(F32) + back[: d.tok]).astype(BF16)

    for j in range(d.owners):
        pl.when(z != d.owner(j))(cast(j, d.owner(j)).wait_recv)

    def gather(i):
        return send(fin.at[tx], fin.at[tx], "gather", i, i, at_tx(lax.rem(tx + i, d.tx)))

    for i in range(1, d.tx):
        start(gather(i))

    proj_z.wait_recv()
    px_v[x] = (pz_v[0].astype(F32) + pz_v[1].astype(F32)).astype(BF16)

    def proj_x(i):
        return send(px_v.at[x], px_v.at[x], "proj_x", i, i, at_x(i))

    for i in range(1, d.x):
        start(proj_x(i))
    for i in range(1, d.x):
        proj_x(i).wait_recv()
    total = px_v[0].astype(F32)
    for i in range(1, d.x):
        total = total + px_v[i].astype(F32)
    proj_out[:, :half] = total[:8]
    proj_out[:, half:] = total[8:]

    for i in range(1, d.tx):
        gather(i).wait_recv()
    out_weight = local(fin, weight_out, 17)

    for when, copy in sent:
        if when is None:
            copy.wait_send()
        else:
            pl.when(when)(copy.wait_send)
    for j in range(d.owners):

        @pl.when(z == d.owner(j))
        def _(j=j):
            for k in range(d.z):
                if k != d.owner(j):
                    cast(j, k).wait_send()

    out_feature.wait()
    out_weight.wait()


def shards(d, *args):
    tile = (d.rows, d.cols, LANES)
    half = 3 * d.width // 2
    blocks = d.width // LANES
    packed = d.tok * blocks
    assert packed == TILE and d.rows == TILE
    _, messages = message_slots(d)
    hbm = pl.BlockSpec(memory_space=pl.ANY)
    vmem = pl.BlockSpec(memory_space=pltpu.VMEM)
    feature_grad, weight_grad, token_grad, proj_grad = pl.pallas_call(
        functools.partial(kernel, d),
        out_shape=(
            jax.ShapeDtypeStruct((1, *tile), BF16),
            jax.ShapeDtypeStruct((d.tx, d.part, LANES), BF16),
            jax.ShapeDtypeStruct((1, d.tok, d.width), BF16),
            jax.ShapeDtypeStruct((8, 3 * d.width), F32),
        ),
        in_specs=[hbm] * 8,
        out_specs=(hbm, hbm, vmem, vmem),
        scratch_shapes=[
            pltpu.VMEM(tile, BF16),
            pltpu.VMEM((d.rows + 2, d.cols, LANES), BF16),
            pltpu.VMEM((d.rows + 2, d.cols, 3 * LANES), BF16),
            pltpu.VMEM((LANES, 9 * LANES), BF16),
            pltpu.VMEM((3, d.width, d.width), BF16),
            pltpu.VMEM(tile, BF16),
            pltpu.VMEM((LANES, 9 * LANES), F32),
            pltpu.VMEM((9 * LANES, LANES), BF16),
            pltpu.VMEM((d.tx, d.part, LANES), BF16),
            pltpu.VMEM((d.x, d.part, LANES), BF16),
            pltpu.VMEM((d.part, LANES), BF16),
            pltpu.VMEM((d.z, d.piece, LANES), BF16),
            pltpu.VMEM((d.tx, d.part, LANES), BF16),
            pltpu.VMEM((2, d.rows, LANES), BF16),
            pltpu.VMEM((2, 3, d.rows, LANES), BF16),
            pltpu.VMEM((2, d.rows + 8, LANES), F32),
            pltpu.VMEM((2, d.tok, d.width), BF16),
            pltpu.VMEM((2, packed, LANES), F32),
            pltpu.VMEM((2, d.tx, d.ty, packed, LANES), BF16),
            pltpu.VMEM((d.tokens * blocks, LANES), F32),
            pltpu.VMEM((2, d.tokens, d.width), BF16),
            pltpu.VMEM((d.tokens, 3 * d.width), BF16),
            pltpu.VMEM((d.tokens, 3 * d.width), BF16),
            pltpu.VMEM((d.zh, 16, half), BF16),
            pltpu.VMEM((d.x, 16, half), BF16),
            pltpu.SemaphoreType.DMA((18,)),
            pltpu.SemaphoreType.DMA((messages,)),
            pltpu.SemaphoreType.DMA((messages,)),
        ],
        compiler_params=pltpu.CompilerParams(
            collective_id=0, has_side_effects=True, vmem_limit_bytes=48 * 1024 * 1024
        ),
    )(*args)
    conv_weight_grad = weight_grad.astype(F32).reshape(3, 3, LANES, LANES)
    return feature_grad, conv_weight_grad, token_grad, proj_grad


def solution(mesh):
    sizes = mesh.shape
    zh = 2

    def whole(*args):
        _, height, width, _ = args[0].shape
        _, tokens, channels = args[3].shape
        d = Dims(
            x=sizes["rep"] // zh,
            zh=zh,
            ty=sizes["ty"],
            tx=sizes["tx"],
            rows=height // sizes["ty"],
            cols=width // sizes["tx"],
            tok=tokens // (sizes["ty"] * sizes["tx"]),
            width=channels,
        )
        in_specs = (
            P("rep", "ty", "tx", None),
            P("rep", "ty", "tx", None),
            P(),
            P("rep", ("ty", "tx"), None),
            P("rep", ("ty", "tx"), None),
            P(),
            P(),
            P(),
        )
        out_specs = (
            P("rep", "ty", "tx", None),
            P(),
            P("rep", ("ty", "tx"), None),
            P(("ty", "tx"), None),
        )
        return jax.shard_map(
            functools.partial(shards, d),
            mesh=mesh,
            in_specs=in_specs,
            out_specs=out_specs,
            check_vma=False,
        )(*args)

    return whole
```

time: 836 us -> 72 us (0.09)
  waiting for transfers between devices: 447 us -> 0 us
  blocking collectives: 312 us -> 0 us
  Pallas kernels: 0 us -> 59.6 us
  matrix products: 28.9 us -> 0 us
  between operations: 14.3 us -> 0.66 us
  starting transfers between devices: 12.5 us -> 0 us
    psum x1 -> x0, waiting for transfers between devices: 447 us -> none  [shards(): lax.psum(weight_part, ('rep', 'ty', 'tx')).reshape(3, 3, chans, chans)]
    all_gather x2 -> x0, blocking collectives: 244 us -> none  [the longest x1 130 us: shards(): lax.all_gather(token_grad, ('ty', 'tx'), axis=0, tiled=True)]
    psum x1 -> x0, blocking collectives: 67.8 us -> none  [shards(): lax.psum(proj_part.astype(jnp.bfloat16), 'rep').astype(jnp.float32)]
    pallas_call x0 -> x1, Pallas kernels: none -> 59.6 us  [shards(): pl.pallas_call(functools.partial(kernel, d), out_shape=(jax.ShapeDtypeStr...]
    dot_general x9 -> x0, matrix products: 25.7 us -> none  [the longest x1 6.25 us: shards(): jnp.dot(grad_cat, flipped, preferred_element_type=jnp.float32)]
    ppermute x4 -> x0, starting transfers between devices: 12.5 us -> none  [the longest x2 9.12 us: padded_2(): before = lax.ppermute(last, axis, up)]
  transfers between devices with their start and end apart: 5 -> 0, of which waited for: 1 -> 0; matrix products, arithmetic and copies ran while one was open for 4% -> 0% of each run, Pallas kernels for 0% -> 0%
where the time goes in v1:
time: 72 us; the launch traced here: 70.9 us
  Pallas kernels  59.6 us (83%)
  local copies, waits for them, and re-layouts  9.81 us (14%)
  other arithmetic  0.86 us (1%)
    pallas_call x1, Pallas kernels, shards(): pl.pallas_call(functools.partial(kernel, d), out_shape=(jax.ShapeDtypeStr...  59.6 us
    unnamed x19, local copies, waits for them, and re-layouts  9.81 us

profile of v1, /device:TPU:1, one launch (start us, length us, event | category | flops | bytes accessed | tf_op | source)
XLA Modules:
  0.0 70.9 jit_solution(11646570673110855956)
XLA Ops:
  0.6 0.0 copy-start
  0.6 1.1 %copy-done = bf16[1,16,192,128]{3,2,1,0:T(8,128)(2,1)S(1)} copy-done((bf16[1,16,192,128]{3,2,1,0:T(8,128)(2,1)S(1)}, bf16[1,16,192,128]{3,2,1,0:T(8,128)(2,1)}, u32[]{:S(2)}) %copy-start) | copy-done | bytes 786456
  1.8 0.0 copy-start.1
  1.8 1.1 %copy-done.1 = bf16[1,16,192,128]{3,2,1,0:T(8,128)(2,1)S(1)} copy-done((bf16[1,16,192,128]{3,2,1,0:T(8,128)(2,1)S(1)}, bf16[1,16,192,128]{3,2,1,0:T(8,128)(2,1)}, u32[]{:S(2)}) %copy-start.1) | copy-done | bytes 786456
  2.9 0.0 copy-start.2
  2.9 1.0 %copy-done.2 = bf16[512,512]{1,0:T(8,128)(2,1)S(1)} copy-done((bf16[512,512]{1,0:T(8,128)(2,1)S(1)}, bf16[512,512]{1,0:T(8,128)(2,1)}, u32[]{:S(2)}) %copy-start.2) | copy-done | bytes 524312
  3.9 0.0 copy-start.3
  3.9 1.0 %copy-done.3 = bf16[512,512]{1,0:T(8,128)(2,1)S(1)} copy-done((bf16[512,512]{1,0:T(8,128)(2,1)S(1)}, bf16[512,512]{1,0:T(8,128)(2,1)}, u32[]{:S(2)}) %copy-start.3) | copy-done | bytes 524312
  5.0 0.0 copy-start.4
  5.0 1.0 %copy-done.4 = bf16[512,512]{1,0:T(8,128)(2,1)S(1)} copy-done((bf16[512,512]{1,0:T(8,128)(2,1)S(1)}, bf16[512,512]{1,0:T(8,128)(2,1)}, u32[]{:S(2)}) %copy-start.4) | copy-done | bytes 524312
  6.0 0.0 copy-start.5
  6.0 1.0 %copy-done.5 = bf16[3,3,128,128]{3,2,1,0:T(8,128)(2,1)S(1)} copy-done((bf16[3,3,128,128]{3,2,1,0:T(8,128)(2,1)S(1)}, bf16[3,3,128,128]{3,2,1,0:T(8,128)(2,1)}, u32[]{:S(2)}) %copy-start.5) | copy-done | bytes 294936
  7.0 0.0 copy-start.6
  7.0 0.7 copy-done.6
  7.7 0.0 copy-start.7
  7.7 0.7 copy-done.7
  8.4 59.6 %shard_map.111 = (bf16[1,16,192,128]{3,2,1,0:T(8,128)(2,1)S(1)}, bf16[8,144,128]{2,1,0:T(8,128)(2,1)S(1)}, bf16[1,4,512]{2,1,0:T(4,128)(2,1)S(1)}, f32[8,1536]{1,0:T(8,128)S(1)}) custom-call(bf16[1,16,192,128]{3,2,1,0:T(8,128)(2,1)S(1)} %copy-done, bf16[1,16,192,128]{3,2,1,0:T(8,128)(2,1)S(1)} %copy-done.1, bf16[3,3,128,128]{3,2,1,0:T(8,128)(2,1)S(1)} %copy-done.5, ...), custom_call_target="tpu_custom_call" | custom-call | tf_op jit(solution)/shard_map/pallas_call | solution.py:524
  67.9 0.9 %convert.1 = f32[3,3,128,128]{3,2,1,0:T(8,128)} convert(bf16[3,3,128,128]{3,2,1,0:T(8,128)(2,1)S(1)} %bitcast.2) | non-fusion elementwise | flops 147456 | bytes 884736 | tf_op jit(solution)/shard_map/reshape | solution.py:568
  68.8 0.9 %copy.15 = bf16[1,16,192,128]{3,2,1,0:T(8,128)(2,1)} copy(bf16[1,16,192,128]{3,2,1,0:T(8,128)(2,1)S(1)} %get-tuple-element.16) | data formatting | bytes 1572864
  69.7 0.6 copy.16
  70.3 0.6 copy.17
Async XLA Ops:
  0.6 1.1 %copy-start = (bf16[1,16,192,128]{3,2,1,0:T(8,128)(2,1)S(1)}, bf16[1,16,192,128]{3,2,1,0:T(8,128)(2,1)}, u32[]{:S(2)}) copy-start(bf16[1,16,192,128]{3,2,1,0:T(8,128)(2,1)} %features.1) | copy-start | bytes 2359300
  1.8 1.1 %copy-start.1 = (bf16[1,16,192,128]{3,2,1,0:T(8,128)(2,1)S(1)}, bf16[1,16,192,128]{3,2,1,0:T(8,128)(2,1)}, u32[]{:S(2)}) copy-start(bf16[1,16,192,128]{3,2,1,0:T(8,128)(2,1)} %fine_grad.1) | copy-start | bytes 2359300
  2.9 1.0 %copy-start.2 = (bf16[512,512]{1,0:T(8,128)(2,1)S(1)}, bf16[512,512]{1,0:T(8,128)(2,1)}, u32[]{:S(2)}) copy-start(bf16[512,512]{1,0:T(8,128)(2,1)} %query_weight.1) | copy-start | bytes 1572868
  3.9 1.0 %copy-start.3 = (bf16[512,512]{1,0:T(8,128)(2,1)S(1)}, bf16[512,512]{1,0:T(8,128)(2,1)}, u32[]{:S(2)}) copy-start(bf16[512,512]{1,0:T(8,128)(2,1)} %key_weight.1) | copy-start | bytes 1572868
  5.0 1.0 %copy-start.4 = (bf16[512,512]{1,0:T(8,128)(2,1)S(1)}, bf16[512,512]{1,0:T(8,128)(2,1)}, u32[]{:S(2)}) copy-start(bf16[512,512]{1,0:T(8,128)(2,1)} %value_weight.1) | copy-start | bytes 1572868
  6.0 1.0 %copy-start.5 = (bf16[3,3,128,128]{3,2,1,0:T(8,128)(2,1)S(1)}, bf16[3,3,128,128]{3,2,1,0:T(8,128)(2,1)}, u32[]{:S(2)}) copy-start(bf16[3,3,128,128]{3,2,1,0:T(8,128)(2,1)} %conv_weight.1) | copy-start | bytes 884740
  7.0 0.7 copy-start.6
  7.7 0.7 copy-start.7

commit v2 on v1

v2 whole, which is shorter than its diff:
```python
import dataclasses
import functools

import jax
import jax.numpy as jnp
from jax import lax
from jax.experimental import pallas as pl
from jax.experimental.pallas import tpu as pltpu
from jax.sharding import PartitionSpec as P

HEAD_DIM = 64
LANES = 128
TILE = 16
CORES = 2
VMEM_LIMIT = 60 * 1024 * 1024
MESH = pl.DeviceIdType.MESH
BF16 = jnp.bfloat16
F32 = jnp.float32

NN = (((1,), (0,)), ((), ()))
NT = (((1,), (1,)), ((), ()))
TN = (((0,), (0,)), ((), ()))


def dot(a, b, dims):
    return lax.dot_general(a, b, dims, preferred_element_type=F32)


@dataclasses.dataclass(frozen=True)
class Dims:
    x: int
    zh: int
    ty: int
    y: int
    rows: int
    cols: int
    tok: int
    width: int

    @property
    def z(self):
        return self.zh * self.ty

    @property
    def tx(self):
        return self.y * CORES

    @property
    def chips(self):
        return self.x * self.y

    @property
    def half(self):
        return 9 * LANES // CORES

    @property
    def owners(self):
        return 12 if self.chips > 12 else self.chips - 1

    @property
    def piece(self):
        return self.half // self.owners

    @property
    def tokens(self):
        return self.ty * self.tx * self.tok


def message_slots(d):
    slots = {}
    count = 0
    for name, n in (
        ("row", 2),
        ("col", 6),
        ("tok_z", d.ty),
        ("tok_y", d.y),
        ("tok_core", 1),
        ("core", 1),
        ("plane", d.chips),
        ("along_z", d.z),
        ("spread", d.chips),
        ("core_back", 1),
        ("proj_z", 1),
        ("proj_x", d.x),
    ):
        slots[name] = count
        count += n
    return slots, count


def kernel(
    d,
    features,
    fine_grad,
    conv_weight,
    bottom,
    bottom_grad,
    query_weight,
    key_weight,
    value_weight,
    feature_out,
    weight_out,
    token_out,
    proj_out,
    feat_v,
    grad_v,
    shifted,
    taps,
    proj_w,
    out_v,
    acc,
    flat,
    core_send,
    core_v,
    half_v,
    plane_v,
    z_v,
    fin,
    col_send,
    col_recv,
    col_halo,
    tok_v,
    pack_v,
    gath,
    wide,
    tok_all,
    qkv,
    pgrad,
    pz_v,
    px_v,
    local_sem,
    send_sem,
    recv_sem,
):
    slots, _ = message_slots(d)
    rows, cols = d.rows, d.cols
    rep, ty, tx = (lax.axis_index(a) for a in ("rep", "ty", "tx"))
    x, zh = rep // d.zh, rep % d.zh
    y, core = tx // CORES, tx % CORES
    z = zh * d.ty + ty
    chip = y * d.x + x

    def at_chip(c):
        return (lax.rem(c, d.x) * d.zh + zh, ty, (c // d.x) * CORES + core)

    def at_z(k):
        return (x * d.zh + k // d.ty, lax.rem(k, d.ty), tx)

    def at_tx(t):
        return (rep, ty, t)

    def at_ty(t):
        return (rep, t, tx)

    other_core = at_tx(y * CORES + 1 - core)

    def send(src, dst, name, out_index, in_index, device):
        return pltpu.make_async_remote_copy(
            src_ref=src,
            dst_ref=dst,
            send_sem=send_sem.at[slots[name] + out_index],
            recv_sem=recv_sem.at[slots[name] + in_index],
            device_id=device,
            device_id_type=MESH,
        )

    sent = []

    def start(copy, when=None):
        sent.append((when, copy))
        if when is None:
            copy.start()
        else:
            pl.when(when)(copy.start)

    def local(src, dst, i):
        copy = pltpu.make_async_copy(src, dst, local_sem.at[i])
        copy.start()
        return copy

    in_tok = [local(bottom.at[0], tok_v.at[0], 0), local(bottom_grad.at[0], tok_v.at[1], 1)]
    in_grad = local(fine_grad.at[0], grad_v.at[pl.ds(1, rows)], 2)
    in_feat = local(features.at[0], feat_v, 3)

    barrier = pltpu.get_barrier_semaphore()
    peers = [other_core]
    peers += [at_tx(lax.rem(tx + i, d.tx)) for i in (1, d.tx - 1)]
    peers += [at_chip(lax.rem(chip + i, d.chips)) for i in range(1, d.chips)]
    peers += [at_z(lax.rem(z + i, d.z)) for i in range(1, d.z)]
    for dy in (1, d.ty - 1):
        for dx in (1, d.tx - 1):
            peers.append((rep, lax.rem(ty + dy, d.ty), lax.rem(tx + dx, d.tx)))
    for peer in peers:
        pl.semaphore_signal(barrier, inc=1, device_id=peer, device_id_type=MESH)

    in_taps = [
        local(conv_weight.at[k // 3, k % 3], taps.at[:, pl.ds(k * LANES, LANES)], 7 + k)
        for k in range(9)
    ]
    in_proj = [
        local(w, proj_w.at[i], 4 + i) for i, w in enumerate((query_weight, key_weight, value_weight))
    ]

    blocks = d.width // LANES
    for i, copy in enumerate(in_tok):
        copy.wait()
        mine = tok_v[i].astype(F32)
        for c in range(blocks):
            pack_v[i, pl.ds(c, d.tok, stride=blocks), :] = mine[:, c * LANES : (c + 1) * LANES]
        gath[core, i, y, ty] = pack_v[i].astype(BF16)
    in_grad.wait()
    lane_rows = lax.broadcasted_iota(jnp.int32, (rows, TILE, LANES), 1)

    def column(ref, first, side):
        base, row = ((0, 0), (cols - TILE, TILE - 1))[side]
        edge = ref[first : first + rows, base : base + TILE, :].astype(F32)
        return jnp.sum(jnp.where(lane_rows == row, edge, 0.0), axis=1)

    for side in range(2):
        col_send[side] = column(grad_v, 1, side).astype(BF16)

    pl.semaphore_wait(barrier, len(peers))

    up, down = ty > 0, ty < d.ty - 1
    left, right = tx > 0, tx < d.tx - 1
    upper, lower = lax.rem(ty + d.ty - 1, d.ty), lax.rem(ty + 1, d.ty)
    row_up = send(grad_v.at[1], grad_v.at[rows + 1], "row", 0, 1, at_ty(upper))
    row_down = send(grad_v.at[rows], grad_v.at[0], "row", 1, 0, at_ty(lower))
    start(row_up, up)
    start(row_down, down)
    arrivals = []
    for side, there, out_ok, in_ok in (
        (0, lax.rem(tx + d.tx - 1, d.tx), left, right),
        (1, lax.rem(tx + 1, d.tx), right, left),
    ):
        for dy, there_y, out_y, in_y in (
            (0, upper, up, down),
            (1, ty, True, True),
            (2, lower, down, up),
        ):
            copy = send(
                col_send.at[side],
                col_recv.at[1 - side, 2 - dy],
                "col",
                side * 3 + dy,
                (1 - side) * 3 + 2 - dy,
                (rep, there_y, there),
            )
            start(copy, jnp.logical_and(out_ok, out_y))
            arrivals.append((jnp.logical_and(in_ok, in_y), copy, 1 - side, 2 - dy))

    def tok_z(i):
        mine = gath.at[core, :, y, ty]
        return send(mine, mine, "tok_z", i, i, at_ty(lax.rem(ty + i, d.ty)))

    for i in range(1, d.ty):
        start(tok_z(i))

    col_halo[...] = jnp.zeros_like(col_halo)
    col_index = lax.broadcasted_iota(jnp.int32, (cols, LANES), 0)

    def shift_row(r, carry):
        line = grad_v[r]
        wide_line = line.astype(F32)
        before = jnp.where(col_index == 0, col_halo[0, pl.ds(r, 1)], pltpu.roll(wide_line, 1, 0))
        after = jnp.where(
            col_index == cols - 1, col_halo[1, pl.ds(r, 1)], pltpu.roll(wide_line, cols - 1, 0)
        )
        shifted[r, :, 0:LANES] = after.astype(BF16)
        shifted[r, :, LANES : 2 * LANES] = line
        shifted[r, :, 2 * LANES :] = before.astype(BF16)
        return carry

    lax.fori_loop(1, rows + 1, shift_row, 0)
    for r in (0, rows + 1):
        shifted[r] = jnp.zeros((cols, 3 * LANES), BF16)
    in_feat.wait()

    group = 4
    pixels = group * cols

    def neighbours(r):
        return jnp.concatenate(
            [
                shifted[pl.ds(r + 2 - ky, group)].reshape(pixels, 3 * LANES)
                for ky in range(3)
            ],
            axis=-1,
        )

    def silu(v):
        value = v.astype(F32)
        return (value * jax.nn.sigmoid(value)).astype(BF16)

    acc[...] = jnp.zeros_like(acc)

    def weight_step(i, carry):
        active = silu(feat_v[pl.ds(i * group, group)].reshape(pixels, LANES))
        acc[...] += dot(active, neighbours(i * group), TN)
        return carry

    lax.fori_loop(0, rows // group, weight_step, 0)

    @pl.when(jnp.logical_not(up))
    def _():
        grad_v[0] = jnp.zeros((cols, LANES), BF16)

    @pl.when(jnp.logical_not(down))
    def _():
        grad_v[rows + 1] = jnp.zeros((cols, LANES), BF16)

    pl.when(up)(row_down.wait_recv)
    pl.when(down)(row_up.wait_recv)
    for ok, copy, side, place in arrivals:

        @pl.when(ok)
        def _(copy=copy, side=side, place=place):
            copy.wait_recv()
            tile = col_recv[side, place].astype(F32)
            if place == 0:
                col_halo[side, 0:1] = tile[rows - 1 : rows]
            elif place == 1:
                col_halo[side, 1 : rows + 1] = tile
            else:
                col_halo[side, rows + 1 : rows + 2] = tile[0:1]

    for r, inner, ky in ((0, 0, 2), (rows + 1, rows - 1, 0)):
        shift_row(r, 0)
        acc[:, ky * 3 * LANES : (ky + 1) * 3 * LANES] += dot(silu(feat_v[inner]), shifted[r], TN)
    halo_row = lax.broadcasted_iota(jnp.int32, (rows + 8, LANES), 0)
    inside = jnp.logical_and(halo_row >= 1, halo_row <= rows)
    for side, kx in ((0, 2), (1, 0)):
        active = silu(column(feat_v, 0, side))
        line = jnp.where(inside, col_halo[side], 0.0)
        three = jnp.concatenate([line[2 - ky : 2 - ky + rows] for ky in range(3)], axis=1)
        more = dot(active, three.astype(BF16), TN)
        for ky in range(3):
            k = ky * 3 + kx
            acc[:, k * LANES : (k + 1) * LANES] += more[:, ky * LANES : (ky + 1) * LANES]
    for k in range(9):
        flat[k * LANES : (k + 1) * LANES, :] = acc[:, k * LANES : (k + 1) * LANES]

    def core_rows(c):
        return pl.ds(pl.multiple_of(c * d.half, TILE), d.half)

    core_send[...] = flat[core_rows(1 - core), :].astype(BF16)
    to_core = send(core_send, core_v, "core", 0, 0, other_core)
    start(to_core)

    tile_row = lax.broadcasted_iota(jnp.int32, (TILE, LANES), 0)

    def fix_row(r, carry):
        for side, base, lanes, row in ((0, 0, 2 * LANES, 0), (1, cols - TILE, 0, TILE - 1)):
            here = (r, pl.ds(base, TILE), pl.ds(lanes, LANES))
            tile = shifted[here].astype(F32)
            tile = jnp.where(tile_row == row, col_halo[side, pl.ds(r, 1)], tile)
            shifted[here] = tile.astype(BF16)
        return carry

    lax.fori_loop(1, rows + 1, fix_row, 0)

    to_core.wait_recv()
    half_v[...] = (flat[core_rows(core), :] + core_v[...].astype(F32)).astype(BF16)
    first = core * (d.chips - d.owners)
    piece = chip - first
    owner = jnp.logical_and(piece >= 0, piece < d.owners)

    def to_plane(p):
        return send(
            half_v.at[pl.ds(p * d.piece, d.piece)],
            plane_v.at[chip],
            "plane",
            p,
            chip,
            at_chip(first + p),
        )

    def from_plane(i):
        there = lax.rem(chip + i, d.chips)
        return send(half_v.at[pl.ds(0, d.piece)], plane_v.at[there], "plane", 0, there, at_chip(there))

    for p in range(d.owners):
        start(to_plane(p), piece != p)

    for i in range(1, d.ty):
        tok_z(i).wait_recv()

    def tok_y(i):
        mine = gath.at[core, :, y]
        return send(mine, mine, "tok_y", i, i, at_tx(lax.rem(tx + i * CORES, d.tx)))

    for i in range(1, d.y):
        start(tok_y(i))

    for copy in in_taps:
        copy.wait()

    def feature_step(i, carry):
        here = pl.ds(i * group, group)
        value = feat_v[here].reshape(pixels, LANES).astype(F32)
        gate = jax.nn.sigmoid(value)
        slope = gate * (1.0 + value * (1.0 - gate))
        act_grad = dot(neighbours(i * group), taps[...], NT)
        upstream = grad_v[pl.ds(i * group + 1, group)].reshape(pixels, LANES).astype(F32)
        out_v[here] = (upstream + slope * act_grad).astype(BF16).reshape(group, cols, LANES)
        return carry

    lax.fori_loop(0, rows // group, feature_step, 0)
    out_feature = local(out_v, feature_out.at[0], 16)

    def along_z(i):
        return send(z_v.at[z], z_v.at[z], "along_z", i, i, at_z(lax.rem(z + i, d.z)))

    @pl.when(owner)
    def _():
        here = pl.ds(pl.multiple_of(piece * d.piece, TILE), d.piece)
        plane_v[chip] = half_v[here, :]
        for i in range(1, d.chips):
            from_plane(i).wait_recv()
        total = plane_v[0].astype(F32)
        for i in range(1, d.chips):
            total = total + plane_v[i].astype(F32)
        z_v[z] = total.astype(BF16)
        for i in range(1, d.z):
            along_z(i).start()

    for i in range(1, d.y):
        tok_y(i).wait_recv()
    to_core_tok = send(gath.at[core], gath.at[core], "tok_core", 0, 0, other_core)
    start(to_core_tok)
    to_core_tok.wait_recv()

    share = d.tokens // CORES
    for c in range(CORES):
        for i in range(2):
            wide[...] = gath[c, i].reshape(share * blocks, LANES).astype(F32)
            for b in range(blocks):
                tok_all[i, c * share : (c + 1) * share, b * LANES : (b + 1) * LANES] = wide[
                    pl.ds(b, share, stride=blocks), :
                ].astype(BF16)
    for i, copy in enumerate(in_proj):
        copy.wait()
        qkv[:, i * d.width : (i + 1) * d.width] = dot(tok_all[0], proj_w[i], NN).astype(BF16)

    lane = lax.broadcasted_iota(jnp.int32, (d.tokens, LANES), 1)
    low = lane < HEAD_DIM
    scale = 1.0 / HEAD_DIM**0.5

    def head_pair(p, carry):
        def block(ref, offset):
            return ref[:, pl.ds(pl.multiple_of(offset + p * LANES, LANES), LANES)]

        def halves(v):
            zero = jnp.zeros_like(v)
            return jnp.concatenate([jnp.where(low, v, zero), jnp.where(low, zero, v)], axis=0)

        key = block(qkv, d.width)
        value = block(qkv, 2 * d.width)
        query2 = halves(block(qkv, 0))
        upstream2 = halves(block(tok_all.at[1], 0))
        scores = dot(key, query2, NT) * scale
        expos = jnp.exp(scores - jnp.max(scores, axis=0, keepdims=True))
        probs = expos / jnp.sum(expos, axis=0, keepdims=True)
        dprobs = dot(value, upstream2, NT)
        dscores = probs * (dprobs - jnp.sum(dprobs * probs, axis=0, keepdims=True))
        dscores_low = (dscores * scale).astype(BF16)
        value_grad = dot(probs.astype(BF16), upstream2, NN)
        key_grad = dot(dscores_low, query2, NN)
        both = dot(dscores_low, key, TN)
        query_grad = jnp.where(low, both[: d.tokens], both[d.tokens :])
        for i, g in enumerate((query_grad, key_grad, value_grad)):
            here = pl.ds(pl.multiple_of(i * d.width + p * LANES, LANES), LANES)
            pgrad[:, here] = g.astype(BF16)
        return carry

    lax.fori_loop(0, d.width // LANES, head_pair, 0)

    place = ((core * d.y + y) * d.ty + ty) * d.tok
    channel = (ty * d.tx + tx) * (d.width // (d.ty * d.tx))
    pick_row = lax.broadcasted_iota(jnp.int32, (2 * 8, d.width), 0)
    pick_col = lax.broadcasted_iota(jnp.int32, (2 * 8, d.width), 1)
    pick = jnp.logical_and(pick_col == channel + pick_row, pick_row < 8).astype(F32).astype(BF16)
    columns = dot(pick, tok_all[0], NT)
    own_row = lax.broadcasted_iota(jnp.int32, (2 * 8, d.tokens), 0)
    own_col = lax.broadcasted_iota(jnp.int32, (2 * 8, d.tokens), 1)
    picked = jnp.where(
        own_row < 8, columns, (own_col == place + own_row - 8).astype(F32)
    ).astype(BF16)
    both = dot(picked, pgrad[...], NN)
    half = 3 * d.width // 2
    pz_v[zh] = jnp.concatenate([both[:8, :half], both[:8, half:]], axis=0).astype(BF16)
    proj_z = send(pz_v.at[zh], pz_v.at[zh], "proj_z", 0, 0, at_z(lax.rem(z + d.ty, d.z)))
    start(proj_z)
    own_grads = both[8:].astype(BF16)
    back = jnp.zeros((8, d.width), F32)
    for i in range(3):
        back = back + dot(own_grads[:, i * d.width : (i + 1) * d.width], proj_w[i], NT)
    token_out[0] = (tok_v[1].astype(F32) + back[: d.tok]).astype(BF16)

    def spread(p, i):
        here = fin.at[core, pl.ds(pl.multiple_of(p * d.piece, TILE), d.piece)]
        return send(here, here, "spread", i, p, at_chip(lax.rem(chip + i, d.chips)))

    @pl.when(owner)
    def _():
        for i in range(1, d.z):
            along_z(i).wait_recv()
        total = z_v[0].astype(F32)
        for i in range(1, d.z):
            total = total + z_v[i].astype(F32)
        fin[core, pl.ds(pl.multiple_of(piece * d.piece, TILE), d.piece)] = total.astype(BF16)
        for i in range(1, d.chips):
            spread(piece, i).start()

    proj_z.wait_recv()
    px_v[x] = (pz_v[0].astype(F32) + pz_v[1].astype(F32)).astype(BF16)

    def proj_x(i):
        return send(
            px_v.at[x], px_v.at[x], "proj_x", i, i, (lax.rem(x + i, d.x) * d.zh + zh, ty, tx)
        )

    for i in range(1, d.x):
        start(proj_x(i))

    for p in range(d.owners):
        pl.when(piece != p)(spread(p, 0).wait_recv)
    back_core = send(fin.at[core], fin.at[core], "core_back", 0, 0, other_core)
    start(back_core)

    for i in range(1, d.x):
        proj_x(i).wait_recv()
    total = px_v[0].astype(F32)
    for i in range(1, d.x):
        total = total + px_v[i].astype(F32)
    proj_out[:, :half] = total[:8]
    proj_out[:, half:] = total[8:]

    back_core.wait_recv()
    out_weight = local(fin, weight_out, 17)

    for when, copy in sent:
        if when is None:
            copy.wait_send()
        else:
            pl.when(when)(copy.wait_send)

    @pl.when(owner)
    def _():
        for i in range(1, d.z):
            along_z(i).wait_send()
        for i in range(1, d.chips):
            spread(piece, i).wait_send()

    out_feature.wait()
    out_weight.wait()


def outputs(d, feature, weight, token, proj, feature_out, weight_out, token_out, proj_out, low, high, sem):
    copies = [
        pltpu.make_async_copy(src, dst, sem.at[i])
        for i, (src, dst) in enumerate(
            ((weight, low), (feature, feature_out), (token, token_out), (proj, proj_out))
        )
    ]
    for copy in copies:
        copy.start()
    copies[0].wait()
    high[...] = low[...].astype(F32)
    copies[0] = pltpu.make_async_copy(high, weight_out, sem.at[0])
    copies[0].start()
    for copy in copies:
        copy.wait()


def shards(d, *args):
    tile = (d.rows, d.cols, LANES)
    half = 3 * d.width // 2
    blocks = d.width // LANES
    packed = d.tok * blocks
    assert packed == TILE and d.rows == TILE
    _, messages = message_slots(d)
    hbm = pl.BlockSpec(memory_space=pl.ANY)
    vmem = pl.BlockSpec(memory_space=pltpu.VMEM)
    results = pl.pallas_call(
        functools.partial(kernel, d),
        out_shape=(
            jax.ShapeDtypeStruct((1, *tile), BF16),
            jax.ShapeDtypeStruct((CORES, d.half, LANES), BF16),
            jax.ShapeDtypeStruct((1, d.tok, d.width), BF16),
            jax.ShapeDtypeStruct((8, 3 * d.width), F32),
        ),
        in_specs=[hbm] * 8,
        out_specs=(hbm, hbm, vmem, vmem),
        scratch_shapes=[
            pltpu.VMEM(tile, BF16),
            pltpu.VMEM((d.rows + 2, d.cols, LANES), BF16),
            pltpu.VMEM((d.rows + 2, d.cols, 3 * LANES), BF16),
            pltpu.VMEM((LANES, 9 * LANES), BF16),
            pltpu.VMEM((3, d.width, d.width), BF16),
            pltpu.VMEM(tile, BF16),
            pltpu.VMEM((LANES, 9 * LANES), F32),
            pltpu.VMEM((9 * LANES, LANES), F32),
            pltpu.VMEM((d.half, LANES), BF16),
            pltpu.VMEM((d.half, LANES), BF16),
            pltpu.VMEM((d.half, LANES), BF16),
            pltpu.VMEM((d.chips, d.piece, LANES), BF16),
            pltpu.VMEM((d.z, d.piece, LANES), BF16),
            pltpu.VMEM((CORES, d.half, LANES), BF16),
            pltpu.VMEM((2, d.rows, LANES), BF16),
            pltpu.VMEM((2, 3, d.rows, LANES), BF16),
            pltpu.VMEM((2, d.rows + 8, LANES), F32),
            pltpu.VMEM((2, d.tok, d.width), BF16),
            pltpu.VMEM((2, packed, LANES), F32),
            pltpu.VMEM((CORES, 2, d.y, d.ty, packed, LANES), BF16),
            pltpu.VMEM((d.tokens * blocks // CORES, LANES), F32),
            pltpu.VMEM((2, d.tokens, d.width), BF16),
            pltpu.VMEM((d.tokens, 3 * d.width), BF16),
            pltpu.VMEM((d.tokens, 3 * d.width), BF16),
            pltpu.VMEM((d.zh, 16, half), BF16),
            pltpu.VMEM((d.x, 16, half), BF16),
            pltpu.SemaphoreType.DMA((18,)),
            pltpu.SemaphoreType.DMA((messages,)),
            pltpu.SemaphoreType.DMA((messages,)),
        ],
        compiler_params=pltpu.CompilerParams(
            collective_id=0, has_side_effects=True, vmem_limit_bytes=VMEM_LIMIT
        ),
    )(*args)
    feature_grad, conv_weight_grad, token_grad, proj_grad = pl.pallas_call(
        functools.partial(outputs, d),
        out_shape=(
            jax.ShapeDtypeStruct((1, *tile), BF16),
            jax.ShapeDtypeStruct((CORES, d.half, LANES), F32),
            jax.ShapeDtypeStruct((1, d.tok, d.width), BF16),
            jax.ShapeDtypeStruct((8, 3 * d.width), F32),
        ),
        in_specs=[hbm] * 4,
        out_specs=(hbm,) * 4,
        scratch_shapes=[
            pltpu.VMEM((CORES, d.half, LANES), BF16),
            pltpu.VMEM((CORES, d.half, LANES), F32),
            pltpu.SemaphoreType.DMA((4,)),
        ],
        compiler_params=pltpu.CompilerParams(vmem_limit_bytes=VMEM_LIMIT),
    )(*results)
    return feature_grad, conv_weight_grad.reshape(3, 3, LANES, LANES), token_grad, proj_grad


def solution(mesh):
    sizes = mesh.shape
    zh = 2

    def whole(*args):
        _, height, width, _ = args[0].shape
        _, tokens, channels = args[3].shape
        d = Dims(
            x=sizes["rep"] // zh,
            zh=zh,
            ty=sizes["ty"],
            y=sizes["tx"] // CORES,
            rows=height // sizes["ty"],
            cols=width // sizes["tx"],
            tok=tokens // (sizes["ty"] * sizes["tx"]),
            width=channels,
        )
        in_specs = (
            P("rep", "ty", "tx", None),
            P("rep", "ty", "tx", None),
            P(),
            P("rep", ("ty", "tx"), None),
            P("rep", ("ty", "tx"), None),
            P(),
            P(),
            P(),
        )
        out_specs = (
            P("rep", "ty", "tx", None),
            P(),
            P("rep", ("ty", "tx"), None),
            P(("ty", "tx"), None),
        )
        return jax.shard_map(
            functools.partial(shards, d),
            mesh=mesh,
            in_specs=in_specs,
            out_specs=out_specs,
            check_vma=False,
        )(*args)

    return whole
```

time: 72 us -> 77.2 us (1.072); the launches traced: 70.9 us -> 77.1 us
  Pallas kernels: 59.6 us -> 76.4 us
  local copies, waits for them, and re-layouts: 9.81 us -> 0 us
  other arithmetic: 0.86 us -> 0 us
    pallas_call x0 -> x1, Pallas kernels: none -> 26.6 us  [shards(): pl.pallas_call(functools.partial(outputs, d), out_shape=(jax.ShapeDtypeSt...]
    unnamed x19 -> x0, local copies, waits for them, and re-layouts: 9.81 us -> none
    pallas_call x1, Pallas kernels: 59.6 us -> 49.8 us  [shards(): pl.pallas_call(functools.partial(kernel, d), out_shape=(jax.ShapeDtypeStr...]
    reshape x1 -> x0, other arithmetic: 0.86 us -> none  [shards(): conv_weight_grad = weight_grad.astype(F32).reshape(3, 3, LANES, LANES)]
where the time goes in v2:
time: 77.2 us; the launch traced here: 77.1 us
  Pallas kernels  76.4 us (99%)
    pallas_call x1, Pallas kernels, shards(): pl.pallas_call(functools.partial(kernel, d), out_shape=(jax.ShapeDtypeStr...  49.8 us
    pallas_call x1, Pallas kernels, shards(): pl.pallas_call(functools.partial(outputs, d), out_shape=(jax.ShapeDtypeSt...  26.6 us

profile of v2, /device:TPU:1, one launch (start us, length us, event | category | flops | bytes accessed | tf_op | source)
XLA Modules:
  0.0 77.1 jit_solution(743156333099060660)
XLA Ops:
  0.6 49.8 %shard_map.111 = (bf16[1,16,192,128]{3,2,1,0:T(8,128)(2,1)}, bf16[2,576,128]{2,1,0:T(8,128)(2,1)}, bf16[1,4,512]{2,1,0:T(4,128)(2,1)}, f32[8,1536]{1,0:T(8,128)}) custom-call(bf16[1,16,192,128]{3,2,1,0:T(8,128)(2,1)} %features.1, bf16[1,16,192,128]{3,2,1,0:T(8,128)(2,1)} %fine_grad.1, bf16[3,3,128,128]{3,2,1,0:T(8,128)(2,1)} %conv_weight.1, ...), custom_call_target="tpu_custom_call" | custom-call | tf_op jit(solution)/shard_map/pallas_call | solution.py:585
  50.5 26.6 %shard_map.112 = (bf16[1,16,192,128]{3,2,1,0:T(8,128)(2,1)}, f32[2,576,128]{2,1,0:T(8,128)}, bf16[1,4,512]{2,1,0:T(4,128)(2,1)}, f32[8,1536]{1,0:T(8,128)}) custom-call(bf16[1,16,192,128]{3,2,1,0:T(8,128)(2,1)} %get-tuple-element.12.feature, bf16[2,576,128]{2,1,0:T(8,128)(2,1)} %get-tuple-element.13.weight, bf16[1,4,512]{2,1,0:T(4,128)(2,1)} %get-tuple-element.14.token, ...), custom_call_target="tpu_custom_call" | custom-call | tf_op jit(solution)/shard_map/pallas_call | solution.py:630

commit v3 on v2

--- a/solution.py
+++ b/solution.py
@@ -12,6 +12,8 @@
 LANES = 128
 TILE = 16
 CORES = 2
+OUT_PARTS = 4
+EARLY = 1
 VMEM_LIMIT = 60 * 1024 * 1024
 MESH = pl.DeviceIdType.MESH
 BF16 = jnp.bfloat16
@@ -54,12 +56,12 @@
         return 9 * LANES // CORES
 
     @property
-    def owners(self):
-        return 12 if self.chips > 12 else self.chips - 1
+    def piece(self):
+        return (self.half // TILE - 1) // self.chips * TILE
 
     @property
-    def piece(self):
-        return self.half // self.owners
+    def extra(self):
+        return self.half // TILE - self.chips * (self.piece // TILE)
 
     @property
     def tokens(self):
@@ -73,12 +75,15 @@
         ("row", 2),
         ("col", 6),
         ("tok_z", d.ty),
-        ("tok_y", d.y),
+        ("tok_y", d.y * d.ty),
         ("tok_core", 1),
         ("core", 1),
         ("plane", d.chips),
         ("along_z", d.z),
         ("spread", d.chips),
+        ("plane_extra", d.chips),
+        ("along_z_extra", d.z),
+        ("spread_extra", d.chips),
         ("core_back", 1),
         ("proj_z", 1),
         ("proj_x", d.x),
@@ -115,6 +120,8 @@
     half_v,
     plane_v,
     z_v,
+    plane_w,
+    z_w,
     fin,
     col_send,
     col_recv,
@@ -218,6 +225,51 @@
 
     for side in range(2):
         col_send[side] = column(grad_v, 1, side).astype(BF16)
+
+    col_halo[...] = jnp.zeros_like(col_halo)
+    col_index = lax.broadcasted_iota(jnp.int32, (cols, LANES), 0)
+
+    def shift_row(r, carry):
+        line = grad_v[r]
+        wide_line = line.astype(F32)
+        before = jnp.where(col_index == 0, col_halo[0, pl.ds(r, 1)], pltpu.roll(wide_line, 1, 0))
+        after = jnp.where(
+            col_index == cols - 1, col_halo[1, pl.ds(r, 1)], pltpu.roll(wide_line, cols - 1, 0)
+        )
+        shifted[r, :, 0:LANES] = after.astype(BF16)
+        shifted[r, :, LANES : 2 * LANES] = line
+        shifted[r, :, 2 * LANES :] = before.astype(BF16)
+        return carry
+
+    lax.fori_loop(1, rows + 1, shift_row, 0)
+    for r in (0, rows + 1):
+        shifted[r] = jnp.zeros((cols, 3 * LANES), BF16)
+    in_feat.wait()
+
+    group = 4
+    pixels = group * cols
+
+    def neighbours(r):
+        return jnp.concatenate(
+            [
+                shifted[pl.ds(r + 2 - ky, group)].reshape(pixels, 3 * LANES)
+                for ky in range(3)
+            ],
+            axis=-1,
+        )
+
+    def silu(v):
+        value = v.astype(F32)
+        return (value * jax.nn.sigmoid(value)).astype(BF16)
+
+    acc[...] = jnp.zeros_like(acc)
+
+    def weight_step(i, carry):
+        active = silu(feat_v[pl.ds(i * group, group)].reshape(pixels, LANES))
+        acc[...] += dot(active, neighbours(i * group), TN)
+        return carry
+
+    lax.fori_loop(0, EARLY, weight_step, 0)
 
     pl.semaphore_wait(barrier, len(peers))
 
@@ -251,55 +303,23 @@
 
     def tok_z(i):
         mine = gath.at[core, :, y, ty]
-        return send(mine, mine, "tok_z", i, i, at_ty(lax.rem(ty + i, d.ty)))
+        return send(mine, mine, "tok_z", i, ty, at_ty(lax.rem(ty + i, d.ty)))
+
+    def tok_z_from(t):
+        there = gath.at[core, :, y, t]
+        return send(there, there, "tok_z", 0, t, at_ty(t))
+
+    def tok_y(i, t):
+        tile = gath.at[core, :, y, t]
+        k = i * d.ty + t
+        return send(tile, tile, "tok_y", k, k, at_tx(lax.rem(tx + i * CORES, d.tx)))
 
     for i in range(1, d.ty):
         start(tok_z(i))
-
-    col_halo[...] = jnp.zeros_like(col_halo)
-    col_index = lax.broadcasted_iota(jnp.int32, (cols, LANES), 0)
-
-    def shift_row(r, carry):
-        line = grad_v[r]
-        wide_line = line.astype(F32)
-        before = jnp.where(col_index == 0, col_halo[0, pl.ds(r, 1)], pltpu.roll(wide_line, 1, 0))
-        after = jnp.where(
-            col_index == cols - 1, col_halo[1, pl.ds(r, 1)], pltpu.roll(wide_line, cols - 1, 0)
-        )
-        shifted[r, :, 0:LANES] = after.astype(BF16)
-        shifted[r, :, LANES : 2 * LANES] = line
-        shifted[r, :, 2 * LANES :] = before.astype(BF16)
-        return carry
-
-    lax.fori_loop(1, rows + 1, shift_row, 0)
-    for r in (0, rows + 1):
-        shifted[r] = jnp.zeros((cols, 3 * LANES), BF16)
-    in_feat.wait()
-
-    group = 4
-    pixels = group * cols
-
-    def neighbours(r):
-        return jnp.concatenate(
-            [
-                shifted[pl.ds(r + 2 - ky, group)].reshape(pixels, 3 * LANES)
-                for ky in range(3)
-            ],
-            axis=-1,
-        )
-
-    def silu(v):
-        value = v.astype(F32)
-        return (value * jax.nn.sigmoid(value)).astype(BF16)
-
-    acc[...] = jnp.zeros_like(acc)
-
-    def weight_step(i, carry):
-        active = silu(feat_v[pl.ds(i * group, group)].reshape(pixels, LANES))
-        acc[...] += dot(active, neighbours(i * group), TN)
-        return carry
-
-    lax.fori_loop(0, rows // group, weight_step, 0)
+    for i in range(1, d.y):
+        tok_y(i, ty).start()
+
+    lax.fori_loop(EARLY, rows // group, weight_step, 0)
 
     @pl.when(jnp.logical_not(up))
     def _():
@@ -361,36 +381,57 @@
 
     to_core.wait_recv()
     half_v[...] = (flat[core_rows(core), :] + core_v[...].astype(F32)).astype(BF16)
-    first = core * (d.chips - d.owners)
-    piece = chip - first
-    owner = jnp.logical_and(piece >= 0, piece < d.owners)
-
-    def to_plane(p):
+
+    spare = lax.rem(chip + core * (d.chips - d.extra), d.chips)
+    has_extra = spare < d.extra
+    last = d.chips * d.piece
+
+    def turned(e):
+        return lax.rem(e + core * d.extra, d.chips)
+
+    def rows_of(c):
+        return pl.ds(pl.multiple_of(c * d.piece, TILE), d.piece)
+
+    def tile_of(e):
+        return pl.ds(pl.multiple_of(last + e * TILE, TILE), TILE)
+
+    def to_plane(i):
+        there = lax.rem(chip + i, d.chips)
         return send(
-            half_v.at[pl.ds(p * d.piece, d.piece)],
-            plane_v.at[chip],
-            "plane",
-            p,
-            chip,
-            at_chip(first + p),
+            half_v.at[rows_of(there)], plane_v.at[chip], "plane", i, chip, at_chip(there)
         )
 
     def from_plane(i):
         there = lax.rem(chip + i, d.chips)
-        return send(half_v.at[pl.ds(0, d.piece)], plane_v.at[there], "plane", 0, there, at_chip(there))
-
-    for p in range(d.owners):
-        start(to_plane(p), piece != p)
-
-    for i in range(1, d.ty):
-        tok_z(i).wait_recv()
-
-    def tok_y(i):
-        mine = gath.at[core, :, y]
-        return send(mine, mine, "tok_y", i, i, at_tx(lax.rem(tx + i * CORES, d.tx)))
-
-    for i in range(1, d.y):
-        start(tok_y(i))
+        return send(
+            half_v.at[rows_of(there)], plane_v.at[there], "plane", i, there, at_chip(there)
+        )
+
+    def to_plane_extra(e):
+        there = turned(e)
+        return send(
+            half_v.at[tile_of(e)], plane_w.at[chip], "plane_extra", e, chip, at_chip(there)
+        )
+
+    def from_plane_extra(i):
+        there = lax.rem(chip + i, d.chips)
+        return send(
+            half_v.at[tile_of(0)], plane_w.at[there], "plane_extra", 0, there, at_chip(there)
+        )
+
+    for i in range(1, d.chips):
+        start(to_plane(i))
+    for e in range(d.extra):
+        start(to_plane_extra(e), spare != e)
+
+    for distance in range(1, d.ty):
+        for t in (ty + distance, ty - distance):
+
+            @pl.when(jnp.logical_and(t >= 0, t < d.ty))
+            def _(t=t):
+                tok_z_from(t).wait_recv()
+                for i in range(1, d.y):
+                    tok_y(i, t).start()
 
     for copy in in_taps:
         copy.wait()
@@ -411,36 +452,54 @@
     def along_z(i):
         return send(z_v.at[z], z_v.at[z], "along_z", i, i, at_z(lax.rem(z + i, d.z)))
 
-    @pl.when(owner)
+    def along_z_extra(i):
+        return send(z_w.at[z], z_w.at[z], "along_z_extra", i, i, at_z(lax.rem(z + i, d.z)))
+
+    def summed(ref, count):
+        total = ref[0].astype(F32)
+        for i in range(1, count):
+            total = total + ref[i].astype(F32)
+        return total.astype(BF16)
+
+    plane_v[chip] = half_v[rows_of(chip), :]
+    for i in range(1, d.chips):
+        from_plane(i).wait_recv()
+    z_v[z] = summed(plane_v, d.chips)
+    for i in range(1, d.z):
+        start(along_z(i))
+
+    @pl.when(has_extra)
     def _():
-        here = pl.ds(pl.multiple_of(piece * d.piece, TILE), d.piece)
-        plane_v[chip] = half_v[here, :]
+        plane_w[chip] = half_v[tile_of(spare), :]
         for i in range(1, d.chips):
-            from_plane(i).wait_recv()
-        total = plane_v[0].astype(F32)
-        for i in range(1, d.chips):
-            total = total + plane_v[i].astype(F32)
-        z_v[z] = total.astype(BF16)
+            from_plane_extra(i).wait_recv()
+        z_w[z] = summed(plane_w, d.chips)
         for i in range(1, d.z):
-            along_z(i).start()
-
-    for i in range(1, d.y):
-        tok_y(i).wait_recv()
+            along_z_extra(i).start()
+
+    for t in range(d.ty):
+        for i in range(1, d.y):
+            tok_y(i, t).wait_recv()
     to_core_tok = send(gath.at[core], gath.at[core], "tok_core", 0, 0, other_core)
     start(to_core_tok)
-    to_core_tok.wait_recv()
 
     share = d.tokens // CORES
-    for c in range(CORES):
+    for copy in in_proj:
+        copy.wait()
+    for c in (core, 1 - core):
+        here = pl.ds(pl.multiple_of(c * share, TILE), share)
+        if c is not core:
+            to_core_tok.wait_recv()
         for i in range(2):
             wide[...] = gath[c, i].reshape(share * blocks, LANES).astype(F32)
             for b in range(blocks):
-                tok_all[i, c * share : (c + 1) * share, b * LANES : (b + 1) * LANES] = wide[
+                tok_all[i, here, b * LANES : (b + 1) * LANES] = wide[
                     pl.ds(b, share, stride=blocks), :
                 ].astype(BF16)
-    for i, copy in enumerate(in_proj):
-        copy.wait()
-        qkv[:, i * d.width : (i + 1) * d.width] = dot(tok_all[0], proj_w[i], NN).astype(BF16)
+        for i in range(3):
+            qkv[here, i * d.width : (i + 1) * d.width] = dot(
+                tok_all[0, here], proj_w[i], NN
+            ).astype(BF16)
 
     lane = lax.broadcasted_iota(jnp.int32, (d.tokens, LANES), 1)
     low = lane < HEAD_DIM
@@ -497,20 +556,27 @@
         back = back + dot(own_grads[:, i * d.width : (i + 1) * d.width], proj_w[i], NT)
     token_out[0] = (tok_v[1].astype(F32) + back[: d.tok]).astype(BF16)
 
-    def spread(p, i):
-        here = fin.at[core, pl.ds(pl.multiple_of(p * d.piece, TILE), d.piece)]
-        return send(here, here, "spread", i, p, at_chip(lax.rem(chip + i, d.chips)))
-
-    @pl.when(owner)
+    def spread(c, i):
+        here = fin.at[core, rows_of(c)]
+        return send(here, here, "spread", i, c, at_chip(lax.rem(chip + i, d.chips)))
+
+    def spread_extra(e, i):
+        here = fin.at[core, tile_of(e)]
+        return send(here, here, "spread_extra", i, e, at_chip(lax.rem(chip + i, d.chips)))
+
+    for i in range(1, d.z):
+        along_z(i).wait_recv()
+    fin[core, rows_of(chip)] = summed(z_v, d.z)
+    for i in range(1, d.chips):
+        start(spread(chip, i))
+
+    @pl.when(has_extra)
     def _():
         for i in range(1, d.z):
-            along_z(i).wait_recv()
-        total = z_v[0].astype(F32)
-        for i in range(1, d.z):
-            total = total + z_v[i].astype(F32)
-        fin[core, pl.ds(pl.multiple_of(piece * d.piece, TILE), d.piece)] = total.astype(BF16)
+            along_z_extra(i).wait_recv()
+        fin[core, tile_of(spare)] = summed(z_w, d.z)
         for i in range(1, d.chips):
-            spread(piece, i).start()
+            spread_extra(spare, i).start()
 
     proj_z.wait_recv()
     px_v[x] = (pz_v[0].astype(F32) + pz_v[1].astype(F32)).astype(BF16)
@@ -523,8 +589,10 @@
     for i in range(1, d.x):
         start(proj_x(i))
 
-    for p in range(d.owners):
-        pl.when(piece != p)(spread(p, 0).wait_recv)
+    for i in range(1, d.chips):
+        spread(lax.rem(chip + i, d.chips), 0).wait_recv()
+    for e in range(d.extra):
+        pl.when(spare != e)(spread_extra(e, 0).wait_recv)
     back_core = send(fin.at[core], fin.at[core], "core_back", 0, 0, other_core)
     start(back_core)
 
@@ -545,31 +613,44 @@
         else:
             pl.when(when)(copy.wait_send)
 
-    @pl.when(owner)
+    @pl.when(has_extra)
     def _():
         for i in range(1, d.z):
-            along_z(i).wait_send()
+            along_z_extra(i).wait_send()
         for i in range(1, d.chips):
-            spread(piece, i).wait_send()
+            spread_extra(spare, i).wait_send()
+
+    for t in range(d.ty):
+        for i in range(1, d.y):
+            tok_y(i, t).wait_send()
 
     out_feature.wait()
     out_weight.wait()
 
 
-def outputs(d, feature, weight, token, proj, feature_out, weight_out, token_out, proj_out, low, high, sem):
-    copies = [
-        pltpu.make_async_copy(src, dst, sem.at[i])
-        for i, (src, dst) in enumerate(
-            ((weight, low), (feature, feature_out), (token, token_out), (proj, proj_out))
-        )
-    ]
-    for copy in copies:
+def outputs(d, feature, weight, token, proj, feature_out, weight_out, token_out, proj_out, *scratch):
+    weight_v, high_v, feature_v, token_v, proj_v, sem_in, sem_out = scratch
+    parts = [(weight, weight_v)]
+    moves = []
+    step = d.rows // OUT_PARTS
+    for i in range(OUT_PARTS):
+        here = pl.ds(i * step, step)
+        moves.append((feature.at[0, here], feature_v.at[here], feature_out.at[0, here]))
+    moves.append((token, token_v, token_out))
+    moves.append((proj, proj_v, proj_out))
+    parts += [m[:2] for m in moves]
+    ins = [pltpu.make_async_copy(a, b, sem_in.at[i]) for i, (a, b) in enumerate(parts)]
+    for copy in ins:
         copy.start()
-    copies[0].wait()
-    high[...] = low[...].astype(F32)
-    copies[0] = pltpu.make_async_copy(high, weight_out, sem.at[0])
-    copies[0].start()
-    for copy in copies:
+    ins[0].wait()
+    high_v[...] = weight_v[...].astype(F32)
+    outs = [pltpu.make_async_copy(high_v, weight_out, sem_out.at[0])]
+    outs[0].start()
+    for i, (_, b, c) in enumerate(moves):
+        ins[i + 1].wait()
+        outs.append(pltpu.make_async_copy(b, c, sem_out.at[i + 1]))
+        outs[-1].start()
+    for copy in outs:
         copy.wait()
 
 
@@ -606,6 +687,8 @@
             pltpu.VMEM((d.half, LANES), BF16),
             pltpu.VMEM((d.chips, d.piece, LANES), BF16),
             pltpu.VMEM((d.z, d.piece, LANES), BF16),
+            pltpu.VMEM((d.chips, TILE, LANES), BF16),
+            pltpu.VMEM((d.z, TILE, LANES), BF16),
             pltpu.VMEM((CORES, d.half, LANES), BF16),
             pltpu.VMEM((2, d.rows, LANES), BF16),
             pltpu.VMEM((2, 3, d.rows, LANES), BF16),
@@ -640,7 +723,11 @@
         scratch_shapes=[
             pltpu.VMEM((CORES, d.half, LANES), BF16),
             pltpu.VMEM((CORES, d.half, LANES), F32),
-            pltpu.SemaphoreType.DMA((4,)),
+            pltpu.VMEM(tile, BF16),
+            pltpu.VMEM((1, d.tok, d.width), BF16),
+            pltpu.VMEM((8, 3 * d.width), F32),
+            pltpu.SemaphoreType.DMA((OUT_PARTS + 3,)),
+            pltpu.SemaphoreType.DMA((OUT_PARTS + 3,)),
         ],
         compiler_params=pltpu.CompilerParams(vmem_limit_bytes=VMEM_LIMIT),
     )(*results)

time: 77.2 us -> 51.7 us (0.67)
  Pallas kernels: 76.4 us -> 50.9 us
    pallas_call x1, Pallas kernels: 26.6 us -> 2.2 us  [shards(): pl.pallas_call(functools.partial(outputs, d), out_shape=(jax.ShapeDtypeSt...]
    pallas_call x1, Pallas kernels: 49.8 us -> 48.7 us  [shards(): pl.pallas_call(functools.partial(kernel, d), out_shape=(jax.ShapeDtypeStr...]
where the time goes in v3:
time: 51.7 us; the launch traced here: 51.5 us
  Pallas kernels  50.9 us (98%)
  between operations  0.64 us (1%)
    pallas_call x1, Pallas kernels, shards(): pl.pallas_call(functools.partial(kernel, d), out_shape=(jax.ShapeDtypeStr...  48.7 us
    pallas_call x1, Pallas kernels, shards(): pl.pallas_call(functools.partial(outputs, d), out_shape=(jax.ShapeDtypeSt...  2.2 us

profile of v3, /device:TPU:1, one launch (start us, length us, event | category | flops | bytes accessed | tf_op | source)
XLA Modules:
  0.0 51.5 jit_solution(17412550491380512426)
XLA Ops:
  0.6 48.7 %shard_map.111 = (bf16[1,16,192,128]{3,2,1,0:T(8,128)(2,1)}, bf16[2,576,128]{2,1,0:T(8,128)(2,1)}, bf16[1,4,512]{2,1,0:T(4,128)(2,1)}, f32[8,1536]{1,0:T(8,128)}) custom-call(bf16[1,16,192,128]{3,2,1,0:T(8,128)(2,1)} %features.1, bf16[1,16,192,128]{3,2,1,0:T(8,128)(2,1)} %fine_grad.1, bf16[3,3,128,128]{3,2,1,0:T(8,128)(2,1)} %conv_weight.1, ...), custom_call_target="tpu_custom_call" | custom-call | tf_op jit(solution)/shard_map/pallas_call | solution.py:666
  49.3 2.2 %shard_map.112 = (bf16[1,16,192,128]{3,2,1,0:T(8,128)(2,1)}, f32[2,576,128]{2,1,0:T(8,128)}, bf16[1,4,512]{2,1,0:T(4,128)(2,1)}, f32[8,1536]{1,0:T(8,128)}) custom-call(bf16[1,16,192,128]{3,2,1,0:T(8,128)(2,1)} %get-tuple-element.12.feature, bf16[2,576,128]{2,1,0:T(8,128)(2,1)} %get-tuple-element.13.weight, bf16[1,4,512]{2,1,0:T(4,128)(2,1)} %get-tuple-element.14.token, ...), custom_call_target="tpu_custom_call" | custom-call | tf_op jit(solution)/shard_map/pallas_call | solution.py:713

commit v4 on v3

--- a/solution.py
+++ b/solution.py
@@ -12,8 +12,7 @@
 LANES = 128
 TILE = 16
 CORES = 2
-OUT_PARTS = 4
-EARLY = 1
+EARLY = 4
 VMEM_LIMIT = 60 * 1024 * 1024
 MESH = pl.DeviceIdType.MESH
 BF16 = jnp.bfloat16
@@ -112,7 +111,6 @@
     shifted,
     taps,
     proj_w,
-    out_v,
     acc,
     flat,
     core_send,
@@ -122,7 +120,6 @@
     z_v,
     plane_w,
     z_w,
-    fin,
     col_send,
     col_recv,
     col_halo,
@@ -193,11 +190,12 @@
     peers = [other_core]
     peers += [at_tx(lax.rem(tx + i, d.tx)) for i in (1, d.tx - 1)]
     peers += [at_chip(lax.rem(chip + i, d.chips)) for i in range(1, d.chips)]
-    peers += [at_z(lax.rem(z + i, d.z)) for i in range(1, d.z)]
+    far = sorted(range(1, d.z), key=lambda i: min(i, d.z - i))
     for dy in (1, d.ty - 1):
         for dx in (1, d.tx - 1):
             peers.append((rep, lax.rem(ty + dy, d.ty), lax.rem(tx + dx, d.tx)))
-    for peer in peers:
+    peers += [at_z(lax.rem(z + i, d.z)) for i in far]
+    for peer in reversed(peers):
         pl.semaphore_signal(barrier, inc=1, device_id=peer, device_id_type=MESH)
 
     in_taps = [
@@ -433,22 +431,6 @@
                 for i in range(1, d.y):
                     tok_y(i, t).start()
 
-    for copy in in_taps:
-        copy.wait()
-
-    def feature_step(i, carry):
-        here = pl.ds(i * group, group)
-        value = feat_v[here].reshape(pixels, LANES).astype(F32)
-        gate = jax.nn.sigmoid(value)
-        slope = gate * (1.0 + value * (1.0 - gate))
-        act_grad = dot(neighbours(i * group), taps[...], NT)
-        upstream = grad_v[pl.ds(i * group + 1, group)].reshape(pixels, LANES).astype(F32)
-        out_v[here] = (upstream + slope * act_grad).astype(BF16).reshape(group, cols, LANES)
-        return carry
-
-    lax.fori_loop(0, rows // group, feature_step, 0)
-    out_feature = local(out_v, feature_out.at[0], 16)
-
     def along_z(i):
         return send(z_v.at[z], z_v.at[z], "along_z", i, i, at_z(lax.rem(z + i, d.z)))
 
@@ -556,17 +538,32 @@
         back = back + dot(own_grads[:, i * d.width : (i + 1) * d.width], proj_w[i], NT)
     token_out[0] = (tok_v[1].astype(F32) + back[: d.tok]).astype(BF16)
 
+    for copy in in_taps:
+        copy.wait()
+
+    def feature_step(i, carry):
+        here = pl.ds(i * group, group)
+        value = feat_v[here].reshape(pixels, LANES).astype(F32)
+        gate = jax.nn.sigmoid(value)
+        slope = gate * (1.0 + value * (1.0 - gate))
+        act_grad = dot(neighbours(i * group), taps[...], NT)
+        upstream = grad_v[pl.ds(i * group + 1, group)].reshape(pixels, LANES).astype(F32)
+        feature_out[0, here] = (upstream + slope * act_grad).astype(BF16).reshape(group, cols, LANES)
+        return carry
+
+    lax.fori_loop(0, rows // group, feature_step, 0)
+
     def spread(c, i):
-        here = fin.at[core, rows_of(c)]
+        here = weight_out.at[core, rows_of(c)]
         return send(here, here, "spread", i, c, at_chip(lax.rem(chip + i, d.chips)))
 
     def spread_extra(e, i):
-        here = fin.at[core, tile_of(e)]
+        here = weight_out.at[core, tile_of(e)]
         return send(here, here, "spread_extra", i, e, at_chip(lax.rem(chip + i, d.chips)))
 
     for i in range(1, d.z):
         along_z(i).wait_recv()
-    fin[core, rows_of(chip)] = summed(z_v, d.z)
+    weight_out[core, rows_of(chip)] = summed(z_v, d.z)
     for i in range(1, d.chips):
         start(spread(chip, i))
 
@@ -574,7 +571,7 @@
     def _():
         for i in range(1, d.z):
             along_z_extra(i).wait_recv()
-        fin[core, tile_of(spare)] = summed(z_w, d.z)
+        weight_out[core, tile_of(spare)] = summed(z_w, d.z)
         for i in range(1, d.chips):
             spread_extra(spare, i).start()
 
@@ -593,7 +590,7 @@
         spread(lax.rem(chip + i, d.chips), 0).wait_recv()
     for e in range(d.extra):
         pl.when(spare != e)(spread_extra(e, 0).wait_recv)
-    back_core = send(fin.at[core], fin.at[core], "core_back", 0, 0, other_core)
+    back_core = send(weight_out.at[core], weight_out.at[core], "core_back", 0, 0, other_core)
     start(back_core)
 
     for i in range(1, d.x):
@@ -605,7 +602,6 @@
     proj_out[:, half:] = total[8:]
 
     back_core.wait_recv()
-    out_weight = local(fin, weight_out, 17)
 
     for when, copy in sent:
         if when is None:
@@ -624,33 +620,19 @@
         for i in range(1, d.y):
             tok_y(i, t).wait_send()
 
-    out_feature.wait()
-    out_weight.wait()
-
-
-def outputs(d, feature, weight, token, proj, feature_out, weight_out, token_out, proj_out, *scratch):
-    weight_v, high_v, feature_v, token_v, proj_v, sem_in, sem_out = scratch
-    parts = [(weight, weight_v)]
-    moves = []
-    step = d.rows // OUT_PARTS
-    for i in range(OUT_PARTS):
-        here = pl.ds(i * step, step)
-        moves.append((feature.at[0, here], feature_v.at[here], feature_out.at[0, here]))
-    moves.append((token, token_v, token_out))
-    moves.append((proj, proj_v, proj_out))
-    parts += [m[:2] for m in moves]
-    ins = [pltpu.make_async_copy(a, b, sem_in.at[i]) for i, (a, b) in enumerate(parts)]
-    for copy in ins:
+
+def outputs(feature, weight, token, proj, feature_out, weight_out, token_out, proj_out, high_v, sem):
+    copies = [
+        pltpu.make_async_copy(src, dst, sem.at[i])
+        for i, (src, dst) in enumerate(
+            ((feature, feature_out), (token, token_out), (proj, proj_out), (high_v, weight_out))
+        )
+    ]
+    for copy in copies[:-1]:
         copy.start()
-    ins[0].wait()
-    high_v[...] = weight_v[...].astype(F32)
-    outs = [pltpu.make_async_copy(high_v, weight_out, sem_out.at[0])]
-    outs[0].start()
-    for i, (_, b, c) in enumerate(moves):
-        ins[i + 1].wait()
-        outs.append(pltpu.make_async_copy(b, c, sem_out.at[i + 1]))
-        outs[-1].start()
-    for copy in outs:
+    high_v[...] = weight[...].astype(F32)
+    copies[-1].start()
+    for copy in copies:
         copy.wait()
 
 
@@ -663,23 +645,23 @@
     _, messages = message_slots(d)
     hbm = pl.BlockSpec(memory_space=pl.ANY)
     vmem = pl.BlockSpec(memory_space=pltpu.VMEM)
+    args = [pltpu.with_memory_space_constraint(a, pltpu.HBM) for a in args]
     results = pl.pallas_call(
         functools.partial(kernel, d),
         out_shape=(
-            jax.ShapeDtypeStruct((1, *tile), BF16),
-            jax.ShapeDtypeStruct((CORES, d.half, LANES), BF16),
-            jax.ShapeDtypeStruct((1, d.tok, d.width), BF16),
-            jax.ShapeDtypeStruct((8, 3 * d.width), F32),
+            pltpu.VMEM((1, *tile), BF16),
+            pltpu.VMEM((CORES, d.half, LANES), BF16),
+            pltpu.VMEM((1, d.tok, d.width), BF16),
+            pltpu.VMEM((8, 3 * d.width), F32),
         ),
         in_specs=[hbm] * 8,
-        out_specs=(hbm, hbm, vmem, vmem),
+        out_specs=(vmem,) * 4,
         scratch_shapes=[
             pltpu.VMEM(tile, BF16),
             pltpu.VMEM((d.rows + 2, d.cols, LANES), BF16),
             pltpu.VMEM((d.rows + 2, d.cols, 3 * LANES), BF16),
             pltpu.VMEM((LANES, 9 * LANES), BF16),
             pltpu.VMEM((3, d.width, d.width), BF16),
-            pltpu.VMEM(tile, BF16),
             pltpu.VMEM((LANES, 9 * LANES), F32),
             pltpu.VMEM((9 * LANES, LANES), F32),
             pltpu.VMEM((d.half, LANES), BF16),
@@ -689,7 +671,6 @@
             pltpu.VMEM((d.z, d.piece, LANES), BF16),
             pltpu.VMEM((d.chips, TILE, LANES), BF16),
             pltpu.VMEM((d.z, TILE, LANES), BF16),
-            pltpu.VMEM((CORES, d.half, LANES), BF16),
             pltpu.VMEM((2, d.rows, LANES), BF16),
             pltpu.VMEM((2, 3, d.rows, LANES), BF16),
             pltpu.VMEM((2, d.rows + 8, LANES), F32),
@@ -702,7 +683,7 @@
             pltpu.VMEM((d.tokens, 3 * d.width), BF16),
             pltpu.VMEM((d.zh, 16, half), BF16),
             pltpu.VMEM((d.x, 16, half), BF16),
-            pltpu.SemaphoreType.DMA((18,)),
+            pltpu.SemaphoreType.DMA((16,)),
             pltpu.SemaphoreType.DMA((messages,)),
             pltpu.SemaphoreType.DMA((messages,)),
         ],
@@ -710,24 +691,20 @@
             collective_id=0, has_side_effects=True, vmem_limit_bytes=VMEM_LIMIT
         ),
     )(*args)
+    results = [pltpu.with_memory_space_constraint(r, pltpu.VMEM) for r in results]
     feature_grad, conv_weight_grad, token_grad, proj_grad = pl.pallas_call(
-        functools.partial(outputs, d),
+        outputs,
         out_shape=(
             jax.ShapeDtypeStruct((1, *tile), BF16),
             jax.ShapeDtypeStruct((CORES, d.half, LANES), F32),
             jax.ShapeDtypeStruct((1, d.tok, d.width), BF16),
             jax.ShapeDtypeStruct((8, 3 * d.width), F32),
         ),
-        in_specs=[hbm] * 4,
+        in_specs=[vmem] * 4,
         out_specs=(hbm,) * 4,
         scratch_shapes=[
-            pltpu.VMEM((CORES, d.half, LANES), BF16),
             pltpu.VMEM((CORES, d.half, LANES), F32),
-            pltpu.VMEM(tile, BF16),
-            pltpu.VMEM((1, d.tok, d.width), BF16),
-            pltpu.VMEM((8, 3 * d.width), F32),
-            pltpu.SemaphoreType.DMA((OUT_PARTS + 3,)),
-            pltpu.SemaphoreType.DMA((OUT_PARTS + 3,)),
+            pltpu.SemaphoreType.DMA((4,)),
         ],
         compiler_params=pltpu.CompilerParams(vmem_limit_bytes=VMEM_LIMIT),
     )(*results)

time: 51.7 us -> 49.4 us (0.956)
  Pallas kernels: 50.9 us -> 48.6 us
    pallas_call x2, Pallas kernels: 50.9 us -> 48.6 us  [the longest x1 47.5 us: shards(): pl.pallas_call(functools.partial(kernel, d), out_shape=(pltpu.VMEM((1, *t...]
where the time goes in v4:
time: 49.4 us; the launch traced here: 49.3 us
  Pallas kernels  48.6 us (98%)
  between operations  0.64 us (1%)
    pallas_call x1, Pallas kernels, shards(): pl.pallas_call(functools.partial(kernel, d), out_shape=(pltpu.VMEM((1, *t...  47.5 us
    pallas_call x1, Pallas kernels, shards(): pl.pallas_call(outputs, out_shape=(jax.ShapeDtypeStruct((1, *tile), BF16)...  1.13 us

profile of v4, /device:TPU:1, one launch (start us, length us, event | category | flops | bytes accessed | tf_op | source)
XLA Modules:
  0.0 49.3 jit_solution(10962092761646321725)
XLA Ops:
  0.6 47.5 %shard_map.111 = (bf16[1,16,192,128]{3,2,1,0:T(8,128)(2,1)S(1)}, bf16[2,576,128]{2,1,0:T(8,128)(2,1)S(1)}, bf16[1,4,512]{2,1,0:T(4,128)(2,1)S(1)}, f32[8,1536]{1,0:T(8,128)S(1)}) custom-call(bf16[1,16,192,128]{3,2,1,0:T(8,128)(2,1)} %features.1, bf16[1,16,192,128]{3,2,1,0:T(8,128)(2,1)} %fine_grad.1, bf16[3,3,128,128]{3,2,1,0:T(8,128)(2,1)} %conv_weight.1, ...), custom_call_target="tpu_custom_call" | custom-call | tf_op jit(solution)/shard_map/pallas_call | solution.py:649
  48.1 1.1 %shard_map.112 = (bf16[1,16,192,128]{3,2,1,0:T(8,128)(2,1)}, f32[2,576,128]{2,1,0:T(8,128)}, bf16[1,4,512]{2,1,0:T(4,128)(2,1)}, f32[8,1536]{1,0:T(8,128)}) custom-call(bf16[1,16,192,128]{3,2,1,0:T(8,128)(2,1)S(1)} %get-tuple-element.12.feature, bf16[2,576,128]{2,1,0:T(8,128)(2,1)S(1)} %get-tuple-element.13.weight, ...), custom_call_target="tpu_custom_call" | custom-call | tf_op jit(solution)/shard_map/pallas_call | solution.py:695

commit v5 on v4

--- a/solution.py
+++ b/solution.py
@@ -84,6 +84,7 @@
         ("along_z_extra", d.z),
         ("spread_extra", d.chips),
         ("core_back", 1),
+        ("heads", 1),
         ("proj_z", 1),
         ("proj_x", d.x),
     ):
@@ -130,6 +131,8 @@
     tok_all,
     qkv,
     pgrad,
+    head_send,
+    head_v,
     pz_v,
     px_v,
     local_sem,
@@ -312,7 +315,7 @@
         k = i * d.ty + t
         return send(tile, tile, "tok_y", k, k, at_tx(lax.rem(tx + i * CORES, d.tx)))
 
-    for i in range(1, d.ty):
+    for i in sorted(range(1, d.ty), key=lambda i: abs(2 * i - d.ty)):
         start(tok_z(i))
     for i in range(1, d.y):
         tok_y(i, ty).start()
@@ -447,7 +450,7 @@
     for i in range(1, d.chips):
         from_plane(i).wait_recv()
     z_v[z] = summed(plane_v, d.chips)
-    for i in range(1, d.z):
+    for i in reversed(far):
         start(along_z(i))
 
     @pl.when(has_extra)
@@ -456,7 +459,7 @@
         for i in range(1, d.chips):
             from_plane_extra(i).wait_recv()
         z_w[z] = summed(plane_w, d.chips)
-        for i in range(1, d.z):
+        for i in reversed(far):
             along_z_extra(i).start()
 
     for t in range(d.ty):
@@ -466,6 +469,8 @@
     start(to_core_tok)
 
     share = d.tokens // CORES
+    heads = d.width // CORES
+    my_heads = pl.ds(pl.multiple_of(core * heads, LANES), heads)
     for copy in in_proj:
         copy.wait()
     for c in (core, 1 - core):
@@ -479,8 +484,8 @@
                     pl.ds(b, share, stride=blocks), :
                 ].astype(BF16)
         for i in range(3):
-            qkv[here, i * d.width : (i + 1) * d.width] = dot(
-                tok_all[0, here], proj_w[i], NN
+            qkv[here, i * heads : (i + 1) * heads] = dot(
+                tok_all[0, here], proj_w[i, :, my_heads], NN
             ).astype(BF16)
 
     lane = lax.broadcasted_iota(jnp.int32, (d.tokens, LANES), 1)
@@ -495,10 +500,10 @@
             zero = jnp.zeros_like(v)
             return jnp.concatenate([jnp.where(low, v, zero), jnp.where(low, zero, v)], axis=0)
 
-        key = block(qkv, d.width)
-        value = block(qkv, 2 * d.width)
+        key = block(qkv, heads)
+        value = block(qkv, 2 * heads)
         query2 = halves(block(qkv, 0))
-        upstream2 = halves(block(tok_all.at[1], 0))
+        upstream2 = halves(block(tok_all.at[1], core * heads))
         scores = dot(key, query2, NT) * scale
         expos = jnp.exp(scores - jnp.max(scores, axis=0, keepdims=True))
         probs = expos / jnp.sum(expos, axis=0, keepdims=True)
@@ -510,32 +515,48 @@
         both = dot(dscores_low, key, TN)
         query_grad = jnp.where(low, both[: d.tokens], both[d.tokens :])
         for i, g in enumerate((query_grad, key_grad, value_grad)):
-            here = pl.ds(pl.multiple_of(i * d.width + p * LANES, LANES), LANES)
+            here = pl.ds(pl.multiple_of(i * heads + p * LANES, LANES), LANES)
             pgrad[:, here] = g.astype(BF16)
         return carry
 
-    lax.fori_loop(0, d.width // LANES, head_pair, 0)
-
-    place = ((core * d.y + y) * d.ty + ty) * d.tok
-    channel = (ty * d.tx + tx) * (d.width // (d.ty * d.tx))
+    lax.fori_loop(0, heads // LANES, head_pair, 0)
+
     pick_row = lax.broadcasted_iota(jnp.int32, (2 * 8, d.width), 0)
     pick_col = lax.broadcasted_iota(jnp.int32, (2 * 8, d.width), 1)
-    pick = jnp.logical_and(pick_col == channel + pick_row, pick_row < 8).astype(F32).astype(BF16)
-    columns = dot(pick, tok_all[0], NT)
     own_row = lax.broadcasted_iota(jnp.int32, (2 * 8, d.tokens), 0)
     own_col = lax.broadcasted_iota(jnp.int32, (2 * 8, d.tokens), 1)
-    picked = jnp.where(
-        own_row < 8, columns, (own_col == place + own_row - 8).astype(F32)
-    ).astype(BF16)
-    both = dot(picked, pgrad[...], NN)
-    half = 3 * d.width // 2
-    pz_v[zh] = jnp.concatenate([both[:8, :half], both[:8, half:]], axis=0).astype(BF16)
-    proj_z = send(pz_v.at[zh], pz_v.at[zh], "proj_z", 0, 0, at_z(lax.rem(z + d.ty, d.z)))
-    start(proj_z)
-    own_grads = both[8:].astype(BF16)
+
+    def rows_for(c):
+        place = ((c * d.y + y) * d.ty + ty) * d.tok
+        channel = (ty * d.tx + y * CORES + c) * (d.width // (d.ty * d.tx))
+        pick = jnp.logical_and(pick_col == channel + pick_row, pick_row < 8).astype(F32)
+        columns = dot(pick.astype(BF16), tok_all[0], NT)
+        picked = jnp.where(own_row < 8, columns, (own_col == place + own_row - 8).astype(F32))
+        return dot(picked.astype(BF16), pgrad[...], NN).astype(BF16)
+
+    head_send[...] = rows_for(1 - core)
+    to_core_heads = send(head_send, head_v.at[core], "heads", 0, 0, other_core)
+    start(to_core_heads)
+    head_v[core] = rows_for(core)
+    to_core_heads.wait_recv()
+    parts = [head_v[c].astype(F32) for c in range(CORES)]
+    px_v[x] = jnp.concatenate([p[:8] for p in parts], axis=0).astype(BF16)
+
+    def proj_x(i):
+        there = (lax.rem(x + i, d.x) * d.zh + zh, ty, tx)
+        return send(px_v.at[x], px_v.at[x], "proj_x", i, i, there)
+
+    for i in range(1, d.x):
+        start(proj_x(i))
     back = jnp.zeros((8, d.width), F32)
-    for i in range(3):
-        back = back + dot(own_grads[:, i * d.width : (i + 1) * d.width], proj_w[i], NT)
+    for c in range(CORES):
+        own_grads = parts[c][8:].astype(BF16)
+        for i in range(3):
+            back = back + dot(
+                own_grads[:, i * heads : (i + 1) * heads],
+                proj_w[i, :, c * heads : (c + 1) * heads],
+                NT,
+            )
     token_out[0] = (tok_v[1].astype(F32) + back[: d.tok]).astype(BF16)
 
     for copy in in_taps:
@@ -553,6 +574,12 @@
 
     lax.fori_loop(0, rows // group, feature_step, 0)
 
+    for i in range(1, d.x):
+        proj_x(i).wait_recv()
+    pz_v[zh] = summed(px_v, d.x)
+    proj_z = send(pz_v.at[zh], pz_v.at[zh], "proj_z", 0, 0, at_z(lax.rem(z + d.ty, d.z)))
+    start(proj_z)
+
     def spread(c, i):
         here = weight_out.at[core, rows_of(c)]
         return send(here, here, "spread", i, c, at_chip(lax.rem(chip + i, d.chips)))
@@ -575,17 +602,6 @@
         for i in range(1, d.chips):
             spread_extra(spare, i).start()
 
-    proj_z.wait_recv()
-    px_v[x] = (pz_v[0].astype(F32) + pz_v[1].astype(F32)).astype(BF16)
-
-    def proj_x(i):
-        return send(
-            px_v.at[x], px_v.at[x], "proj_x", i, i, (lax.rem(x + i, d.x) * d.zh + zh, ty, tx)
-        )
-
-    for i in range(1, d.x):
-        start(proj_x(i))
-
     for i in range(1, d.chips):
         spread(lax.rem(chip + i, d.chips), 0).wait_recv()
     for e in range(d.extra):
@@ -593,13 +609,14 @@
     back_core = send(weight_out.at[core], weight_out.at[core], "core_back", 0, 0, other_core)
     start(back_core)
 
-    for i in range(1, d.x):
-        proj_x(i).wait_recv()
-    total = px_v[0].astype(F32)
-    for i in range(1, d.x):
-        total = total + px_v[i].astype(F32)
-    proj_out[:, :half] = total[:8]
-    proj_out[:, half:] = total[8:]
+    proj_z.wait_recv()
+    total = pz_v[0].astype(F32)
+    for k in range(1, d.zh):
+        total = total + pz_v[k].astype(F32)
+    for i in range(3):
+        for c in range(CORES):
+            first = i * d.width + c * heads
+            proj_out[:, first : first + heads] = total[c * 8 : c * 8 + 8, i * heads : (i + 1) * heads]
 
     back_core.wait_recv()
 
@@ -679,8 +696,10 @@
             pltpu.VMEM((CORES, 2, d.y, d.ty, packed, LANES), BF16),
             pltpu.VMEM((d.tokens * blocks // CORES, LANES), F32),
             pltpu.VMEM((2, d.tokens, d.width), BF16),
-            pltpu.VMEM((d.tokens, 3 * d.width), BF16),
-            pltpu.VMEM((d.tokens, 3 * d.width), BF16),
+            pltpu.VMEM((d.tokens, half), BF16),
+            pltpu.VMEM((d.tokens, half), BF16),
+            pltpu.VMEM((2 * 8, half), BF16),
+            pltpu.VMEM((CORES, 2 * 8, half), BF16),
             pltpu.VMEM((d.zh, 16, half), BF16),
             pltpu.VMEM((d.x, 16, half), BF16),
             pltpu.SemaphoreType.DMA((16,)),

time: 49.4 us -> 48.8 us (0.988)
  Pallas kernels: 48.6 us -> 48 us
    pallas_call x1, Pallas kernels: 47.5 us -> 46.9 us  [shards(): pl.pallas_call(functools.partial(kernel, d), out_shape=(pltpu.VMEM((1, *t...]
where the time goes in v5:
time: 48.8 us; the launch traced here: 48.6 us
  Pallas kernels  48 us (98%)
  between operations  0.64 us (1%)
    pallas_call x1, Pallas kernels, shards(): pl.pallas_call(functools.partial(kernel, d), out_shape=(pltpu.VMEM((1, *t...  46.9 us
    pallas_call x1, Pallas kernels, shards(): pl.pallas_call(outputs, out_shape=(jax.ShapeDtypeStruct((1, *tile), BF16)...  1.13 us

profile of v5, /device:TPU:1, one launch (start us, length us, event | category | flops | bytes accessed | tf_op | source)
XLA Modules:
  0.0 48.6 jit_solution(14319821044676252422)
XLA Ops:
  0.6 46.9 %shard_map.111 = (bf16[1,16,192,128]{3,2,1,0:T(8,128)(2,1)S(1)}, bf16[2,576,128]{2,1,0:T(8,128)(2,1)S(1)}, bf16[1,4,512]{2,1,0:T(4,128)(2,1)S(1)}, f32[8,1536]{1,0:T(8,128)S(1)}) custom-call(bf16[1,16,192,128]{3,2,1,0:T(8,128)(2,1)} %features.1, bf16[1,16,192,128]{3,2,1,0:T(8,128)(2,1)} %fine_grad.1, bf16[3,3,128,128]{3,2,1,0:T(8,128)(2,1)} %conv_weight.1, ...), custom_call_target="tpu_custom_call" | custom-call | tf_op jit(solution)/shard_map/pallas_call | solution.py:666
  47.5 1.1 %shard_map.112 = (bf16[1,16,192,128]{3,2,1,0:T(8,128)(2,1)}, f32[2,576,128]{2,1,0:T(8,128)}, bf16[1,4,512]{2,1,0:T(4,128)(2,1)}, f32[8,1536]{1,0:T(8,128)}) custom-call(bf16[1,16,192,128]{3,2,1,0:T(8,128)(2,1)S(1)} %get-tuple-element.12.feature, bf16[2,576,128]{2,1,0:T(8,128)(2,1)S(1)} %get-tuple-element.13.weight, ...), custom_call_target="tpu_custom_call" | custom-call | tf_op jit(solution)/shard_map/pallas_call | solution.py:714

commit v6 on v5

--- a/solution.py
+++ b/solution.py
@@ -12,7 +12,6 @@
 LANES = 128
 TILE = 16
 CORES = 2
-EARLY = 4
 VMEM_LIMIT = 60 * 1024 * 1024
 MESH = pl.DeviceIdType.MESH
 BF16 = jnp.bfloat16
@@ -114,6 +113,8 @@
     proj_w,
     acc,
     flat,
+    edge_row,
+    edge_col,
     core_send,
     core_v,
     half_v,
@@ -161,6 +162,16 @@
 
     other_core = at_tx(y * CORES + 1 - core)
 
+    def away(o):
+        return min(o[0], d.y - o[0]) + min(o[1], d.x - o[1])
+
+    offsets = [(dy, dx) for dy in range(d.y) for dx in range(d.x) if (dy, dx) != (0, 0)]
+    offsets.sort(key=away, reverse=True)
+
+    def beside(i):
+        dy, dx = offsets[i - 1]
+        return lax.rem(y + dy, d.y) * d.x + lax.rem(x + dx, d.x)
+
     def send(src, dst, name, out_index, in_index, device):
         return pltpu.make_async_remote_copy(
             src_ref=src,
@@ -192,7 +203,7 @@
     barrier = pltpu.get_barrier_semaphore()
     peers = [other_core]
     peers += [at_tx(lax.rem(tx + i, d.tx)) for i in (1, d.tx - 1)]
-    peers += [at_chip(lax.rem(chip + i, d.chips)) for i in range(1, d.chips)]
+    peers += [at_chip(beside(i)) for i in range(1, d.chips)]
     far = sorted(range(1, d.z), key=lambda i: min(i, d.z - i))
     for dy in (1, d.ty - 1):
         for dx in (1, d.tx - 1):
@@ -270,7 +281,12 @@
         acc[...] += dot(active, neighbours(i * group), TN)
         return carry
 
-    lax.fori_loop(0, EARLY, weight_step, 0)
+    lax.fori_loop(0, rows // group, weight_step, 0)
+    for k in range(9):
+        flat[k * LANES : (k + 1) * LANES, :] = acc[:, k * LANES : (k + 1) * LANES]
+    for side in range(2):
+        edge_row[side] = silu(feat_v[(0, rows - 1)[side]])
+        edge_col[side] = silu(column(feat_v, 0, side))
 
     pl.semaphore_wait(barrier, len(peers))
 
@@ -320,8 +336,6 @@
     for i in range(1, d.y):
         tok_y(i, ty).start()
 
-    lax.fori_loop(EARLY, rows // group, weight_step, 0)
-
     @pl.when(jnp.logical_not(up))
     def _():
         grad_v[0] = jnp.zeros((cols, LANES), BF16)
@@ -345,21 +359,22 @@
             else:
                 col_halo[side, rows + 1 : rows + 2] = tile[0:1]
 
-    for r, inner, ky in ((0, 0, 2), (rows + 1, rows - 1, 0)):
+    def add(k, term):
+        flat[k * LANES : (k + 1) * LANES, :] += term
+
+    for side, r, ky in ((0, 0, 2), (1, rows + 1, 0)):
         shift_row(r, 0)
-        acc[:, ky * 3 * LANES : (ky + 1) * 3 * LANES] += dot(silu(feat_v[inner]), shifted[r], TN)
+        more = dot(edge_row[side], shifted[r], TN)
+        for kx in range(3):
+            add(ky * 3 + kx, more[:, kx * LANES : (kx + 1) * LANES])
     halo_row = lax.broadcasted_iota(jnp.int32, (rows + 8, LANES), 0)
     inside = jnp.logical_and(halo_row >= 1, halo_row <= rows)
     for side, kx in ((0, 2), (1, 0)):
-        active = silu(column(feat_v, 0, side))
         line = jnp.where(inside, col_halo[side], 0.0)
         three = jnp.concatenate([line[2 - ky : 2 - ky + rows] for ky in range(3)], axis=1)
-        more = dot(active, three.astype(BF16), TN)
+        more = dot(edge_col[side], three.astype(BF16), TN)
         for ky in range(3):
-            k = ky * 3 + kx
-            acc[:, k * LANES : (k + 1) * LANES] += more[:, ky * LANES : (ky + 1) * LANES]
-    for k in range(9):
-        flat[k * LANES : (k + 1) * LANES, :] = acc[:, k * LANES : (k + 1) * LANES]
+            add(ky * 3 + kx, more[:, ky * LANES : (ky + 1) * LANES])
 
     def core_rows(c):
         return pl.ds(pl.multiple_of(c * d.half, TILE), d.half)
@@ -397,13 +412,13 @@
         return pl.ds(pl.multiple_of(last + e * TILE, TILE), TILE)
 
     def to_plane(i):
-        there = lax.rem(chip + i, d.chips)
+        there = beside(i)
         return send(
             half_v.at[rows_of(there)], plane_v.at[chip], "plane", i, chip, at_chip(there)
         )
 
     def from_plane(i):
-        there = lax.rem(chip + i, d.chips)
+        there = beside(i)
         return send(
             half_v.at[rows_of(there)], plane_v.at[there], "plane", i, there, at_chip(there)
         )
@@ -415,7 +430,7 @@
         )
 
     def from_plane_extra(i):
-        there = lax.rem(chip + i, d.chips)
+        there = beside(i)
         return send(
             half_v.at[tile_of(0)], plane_w.at[there], "plane_extra", 0, there, at_chip(there)
         )
@@ -582,11 +597,11 @@
 
     def spread(c, i):
         here = weight_out.at[core, rows_of(c)]
-        return send(here, here, "spread", i, c, at_chip(lax.rem(chip + i, d.chips)))
+        return send(here, here, "spread", i, c, at_chip(beside(i)))
 
     def spread_extra(e, i):
         here = weight_out.at[core, tile_of(e)]
-        return send(here, here, "spread_extra", i, e, at_chip(lax.rem(chip + i, d.chips)))
+        return send(here, here, "spread_extra", i, e, at_chip(beside(i)))
 
     for i in range(1, d.z):
         along_z(i).wait_recv()
@@ -603,7 +618,7 @@
             spread_extra(spare, i).start()
 
     for i in range(1, d.chips):
-        spread(lax.rem(chip + i, d.chips), 0).wait_recv()
+        spread(beside(i), 0).wait_recv()
     for e in range(d.extra):
         pl.when(spare != e)(spread_extra(e, 0).wait_recv)
     back_core = send(weight_out.at[core], weight_out.at[core], "core_back", 0, 0, other_core)
@@ -681,6 +696,8 @@
             pltpu.VMEM((3, d.width, d.width), BF16),
             pltpu.VMEM((LANES, 9 * LANES), F32),
             pltpu.VMEM((9 * LANES, LANES), F32),
+            pltpu.VMEM((2, d.cols, LANES), BF16),
+            pltpu.VMEM((2, d.rows, LANES), BF16),
             pltpu.VMEM((d.half, LANES), BF16),
             pltpu.VMEM((d.half, LANES), BF16),
             pltpu.VMEM((d.half, LANES), BF16),

time: 48.8 us -> 48.5 us (level)
  no operation moved by 1% of the time
where the time goes in v6:
time: 48.5 us; the launch traced here: 48.3 us
  Pallas kernels  47.7 us (98%)
  between operations  0.64 us (1%)
    pallas_call x1, Pallas kernels, shards(): pl.pallas_call(functools.partial(kernel, d), out_shape=(pltpu.VMEM((1, *t...  46.6 us
    pallas_call x1, Pallas kernels, shards(): pl.pallas_call(outputs, out_shape=(jax.ShapeDtypeStruct((1, *tile), BF16)...  1.13 us

profile of v6, /device:TPU:1, one launch (start us, length us, event | category | flops | bytes accessed | tf_op | source)
XLA Modules:
  0.0 48.3 jit_solution(12032015126024436669)
XLA Ops:
  0.6 46.6 %shard_map.111 = (bf16[1,16,192,128]{3,2,1,0:T(8,128)(2,1)S(1)}, bf16[2,576,128]{2,1,0:T(8,128)(2,1)S(1)}, bf16[1,4,512]{2,1,0:T(4,128)(2,1)S(1)}, f32[8,1536]{1,0:T(8,128)S(1)}) custom-call(bf16[1,16,192,128]{3,2,1,0:T(8,128)(2,1)} %features.1, bf16[1,16,192,128]{3,2,1,0:T(8,128)(2,1)} %fine_grad.1, bf16[3,3,128,128]{3,2,1,0:T(8,128)(2,1)} %conv_weight.1, ...), custom_call_target="tpu_custom_call" | custom-call | tf_op jit(solution)/shard_map/pallas_call | solution.py:681
  47.2 1.1 %shard_map.112 = (bf16[1,16,192,128]{3,2,1,0:T(8,128)(2,1)}, f32[2,576,128]{2,1,0:T(8,128)}, bf16[1,4,512]{2,1,0:T(4,128)(2,1)}, f32[8,1536]{1,0:T(8,128)}) custom-call(bf16[1,16,192,128]{3,2,1,0:T(8,128)(2,1)S(1)} %get-tuple-element.12.feature, bf16[2,576,128]{2,1,0:T(8,128)(2,1)S(1)} %get-tuple-element.13.weight, ...), custom_call_target="tpu_custom_call" | custom-call | tf_op jit(solution)/shard_map/pallas_call | solution.py:731
